TPU v7x, 256 devices: a whole 4x4x8 slice. The times are simulated.
256 devices in a mesh: pb: 8 (over z_lo, y), ka: 32 (over z_hi, x, core).
Axes of the slice: x: 4, y: 4, z: 8 (z_hi: 4, z_lo: 2; z = z_hi * 2 + z_lo), core: 2. Of those that a mesh axis runs over, the one named last changes fastest.
Arguments:
- query_features: bfloat16 [32768, 128], P(('pb', 'ka')), may hold values from -240 to 240, as said below
- key_features: bfloat16 [131072, 128], P(('ka', 'pb')), may hold values from -16 to 16, as said below
Outputs:
- forward_flow: float32 [2, 32768], P(None, ('pb', 'ka'))
- backward_flow: float32 [2, 131072], P(None, ('ka', 'pb'))
Inputs may be any that keep to these rules, and one draw needn't show every extreme that they name: `query_features`: finite feature values. `key_features`: finite feature values.
All inputs are finite; a program needn't handle non-finite values.
Results may differ from a plain program's by a relative error of at most 0.0009.
Values may be sent and summed in bfloat16 or wider, within the bound.
No kernel may reach another device: no remote copies, remote signals or barrier semaphores. Data moves between devices by JAX's collectives and lax.ppermute only.
A program may use at most 192 MiB of HBM per device.

v0:
```python
import jax
import jax.numpy as jnp
from jax import lax
from jax.sharding import PartitionSpec as P

FRAME_W = 480


def joined(value, axis, join):
    pieces = jax.tree.map(lambda part: lax.all_gather(part, axis), value)
    head = jax.tree.map(lambda part: part[0], pieces)
    tail = jax.tree.map(lambda part: part[1:], pieces)
    subtotal, _ = lax.scan(lambda subtotal, piece: (join(subtotal, piece), None), head, tail)
    return subtotal


def combine_stats(left, right):
    top = jnp.maximum(left[0], right[0])
    left_w = jnp.exp(left[0] - top)
    right_w = jnp.exp(right[0] - top)
    return (
        top,
        left[1] * left_w + right[1] * right_w,
        left[2] * left_w + right[2] * right_w,
        left[3] * left_w + right[3] * right_w,
    )


def cell_position(index):
    return (
        (index % FRAME_W).astype(jnp.float32) / FRAME_W,
        (index // FRAME_W).astype(jnp.float32) / FRAME_W,
    )


def on_device(query_features, key_features):
    queries = lax.all_gather(query_features, "ka", axis=0, tiled=True)
    keys = lax.all_gather(key_features, "pb", axis=0, tiled=True)
    query_count, channels = queries.shape
    key_count = keys.shape[0]
    scale = 1.0 / channels**0.5
    query_base = lax.axis_index("pb") * query_count
    key_base = lax.axis_index("ka") * key_count
    key_x, key_y = cell_position(key_base + jnp.arange(key_count, dtype=jnp.int32))
    block = min(512, query_count)
    col_max = jnp.full((key_count,), -jnp.inf, jnp.float32)
    col_sum = jnp.zeros((key_count,), jnp.float32)
    col_x = jnp.zeros((key_count,), jnp.float32)
    col_y = jnp.zeros((key_count,), jnp.float32)
    row_parts = []
    for number in range(query_count // block):
        rows = queries[number * block : (number + 1) * block]
        query_x, query_y = cell_position(
            query_base + number * block + jnp.arange(block, dtype=jnp.int32)
        )
        score = (
            lax.dot_general(
                rows, keys, (((1,), (1,)), ((), ())), preferred_element_type=jnp.float32
            )
            * scale
        )
        row_max = jnp.max(score, axis=1)
        weights = jnp.exp(score - row_max[:, None])
        row_parts.append(
            (
                row_max,
                jnp.sum(weights, axis=1),
                jnp.sum(weights * key_x[None, :], axis=1),
                jnp.sum(weights * key_y[None, :], axis=1),
            )
        )
        top = jnp.maximum(col_max, jnp.max(score, axis=0))
        factor = jnp.exp(col_max - top)
        col_weights = jnp.exp(score - top[None, :])
        col_sum = col_sum * factor + jnp.sum(col_weights, axis=0)
        col_x = col_x * factor + jnp.sum(col_weights * query_x[:, None], axis=0)
        col_y = col_y * factor + jnp.sum(col_weights * query_y[:, None], axis=0)
        col_max = top
    row_max = jnp.concatenate([part[0] for part in row_parts])
    row_sum = jnp.concatenate([part[1] for part in row_parts])
    row_x = jnp.concatenate([part[2] for part in row_parts])
    row_y = jnp.concatenate([part[3] for part in row_parts])
    query_share = query_count // lax.axis_size("ka")
    query_start = lax.axis_index("ka") * query_share
    key_share = key_count // lax.axis_size("pb")
    key_start = lax.axis_index("pb") * key_share
    merged_rows = joined((row_max, row_sum, row_x, row_y), "ka", combine_stats)
    own_sum = lax.dynamic_slice_in_dim(merged_rows[1], query_start, query_share, 0)
    own_x = lax.dynamic_slice_in_dim(merged_rows[2], query_start, query_share, 0)
    own_y = lax.dynamic_slice_in_dim(merged_rows[3], query_start, query_share, 0)
    merged_cols = joined((col_max, col_sum, col_x, col_y), "pb", combine_stats)
    key_sum = lax.dynamic_slice_in_dim(merged_cols[1], key_start, key_share, 0)
    key_wx = lax.dynamic_slice_in_dim(merged_cols[2], key_start, key_share, 0)
    key_wy = lax.dynamic_slice_in_dim(merged_cols[3], key_start, key_share, 0)
    own_qx, own_qy = cell_position(
        query_base + query_start + jnp.arange(query_share, dtype=jnp.int32)
    )
    forward_flow = jnp.stack([own_x / own_sum - own_qx, own_y / own_sum - own_qy])
    own_kx, own_ky = cell_position(key_base + key_start + jnp.arange(key_share, dtype=jnp.int32))
    backward_flow = jnp.stack([key_wx / key_sum - own_kx, key_wy / key_sum - own_ky])
    return (forward_flow, backward_flow)


def solution(mesh):
    return jax.shard_map(
        on_device,
        mesh=mesh,
        in_specs=(P(("pb", "ka"), None), P(("ka", "pb"), None)),
        out_specs=(P(None, ("pb", "ka")), P(None, ("ka", "pb"))),
        check_vma=False,
    )
```

profile of v0, /device:TPU:1, one launch (start us, length us, event | category | flops | bytes accessed | tf_op | source)
XLA Modules:
  0.0 497.8 jit_solution(11738887521676480828)
XLA Ops:
  7.9 0.7 all-gather.11.cloned.1.call-update
  8.9 41.3 %all-gather.13.cloned.1.call-done = bf16[4096,128]{1,0:T(8,128)(2,1)} async-done(((bf16[512,128]{1,0:T(8,128)(2,1)}), bf16[4096,128]{1,0:T(8,128)(2,1)}) %all-gather.13.cloned.1.call-update) | async-done | bytes 1048592 | tf_op jit(solution)/shard_map/all_gather | solution.py:38
  50.3 59.0 %all-gather.11.cloned.1.call-done = bf16[4096,128]{1,0:T(8,128)(2,1)} async-done(((bf16[128,128]{1,0:T(8,128)(2,1)}), bf16[4096,128]{1,0:T(8,128)(2,1)}) %all-gather.11.cloned.1.call-update) | async-done | bytes 1048592 | tf_op jit(solution)/shard_map/all_gather | solution.py:37
  109.3 5.9 %multiply_reduce_fusion.46 = (f32[4096]{0:T(1024)S(1)}, f32[512]{0:T(512)S(1)}, f32[512,4096]{1,0:T(8,128)}) fusion(bf16[4096,128]{1,0:T(8,128)(2,1)} %all-gather.13.cloned.1.call-done, bf16[4096,128]{1,0:T(8,128)(2,1)} %all-gather.11.cloned.1.call-done), kind=kOutput, calls=%fused_computation.80 | convolution fusion | flops 543157760 | bytes 9586688 | tf_op jit(solution)/shard_map/dot_general | solution.py:57
  115.1 1.3 multiply_reduce_fusion.38
  116.5 1.3 multiply_reduce_fusion.44
  117.8 1.3 multiply_reduce_fusion.42
  119.2 4.5 multiply_reduce_fusion.40
  123.6 4.5 multiply_reduce_fusion.36
  128.1 4.5 multiply_reduce_fusion.34
  132.6 1.3 multiply_reduce_fusion.32
  134.0 17.6 %multiply_reduce_fusion.2 = (f32[4096]{0:T(1024)S(1)}, f32[4096]{0:T(1024)S(1)}, f32[4096]{0:T(1024)S(1)}, f32[512]{0:T(512)S(1)}, f32[512]{0:T(512)S(1)}, /*ind...) fusion(f32[512,4096]{1,0:T(8,128)} %get-tuple-element.298, ...), kind=kLoop, calls=%fused_computation.20 | loop fusion | flops 54498304 | bytes 16965632 | tf_op jit(solution)/shard_map/reduce_sum | solution.py:77
  151.6 25.8 %multiply_reduce_fusion.1 = (f32[4096]{0:T(1024)S(1)}, f32[4096]{0:T(1024)S(1)}, f32[4096]{0:T(1024)S(1)}, f32[512]{0:T(512)S(1)}, f32[512]{0:T(512)S(1)}, /*ind...) fusion(f32[512,4096]{1,0:T(8,128)} %get-tuple-element.299, ...), kind=kLoop, calls=%fused_computation.19 | loop fusion | flops 81747456 | bytes 25432064 | tf_op jit(solution)/shard_map/reduce_sum | solution.py:77
  177.4 23.7 %multiply_reduce_fusion = (f32[4096]{0:T(1024)S(1)}, f32[4096]{0:T(1024)S(1)}, f32[4096]{0:T(1024)S(1)}, f32[512]{0:T(512)S(1)}, f32[512]{0:T(512)S(1)}, /*index...) fusion(f32[512,4096]{1,0:T(8,128)S(1)} %get-tuple-element.300, ...), kind=kLoop, calls=%fused_computation.18 | loop fusion | flops 81747456 | bytes 25432064 | tf_op jit(solution)/shard_map/reduce_sum | solution.py:77
  201.5 22.2 %all-gather.5 = f32[8,1,4096]{2,1,0:T(1,128)S(1)} all-gather(f32[1,1,4096]{2,1,0:T(1,128)S(1)} %add_bitcast_fusion.2), channel_id=1, replica_groups=mesh['pb'=8,'ka'=32] {'pb'}, dimensions={0}, use_global_device_ids=true | all-gather | bytes 147456 | tf_op jit(solution)/shard_map/all_gather | solution.py:10
  223.9 21.8 %all-gather.4 = f32[8,1,4096]{2,1,0:T(1,128)S(1)} all-gather(f32[1,1,4096]{2,1,0:T(1,128)S(1)} %get-tuple-element.258), channel_id=1, replica_groups=mesh['pb'=8,'ka'=32] {'pb'}, dimensions={0}, use_global_device_ids=true | all-gather | bytes 147456 | tf_op jit(solution)/shard_map/all_gather | solution.py:10
  245.7 21.8 %all-gather.6 = f32[8,1,4096]{2,1,0:T(1,128)S(1)} all-gather(f32[1,1,4096]{2,1,0:T(1,128)S(1)} %get-tuple-element.257), channel_id=1, replica_groups=mesh['pb'=8,'ka'=32] {'pb'}, dimensions={0}, use_global_device_ids=true | all-gather | bytes 147456 | tf_op jit(solution)/shard_map/all_gather | solution.py:10
  267.6 21.8 %all-gather.7 = f32[8,1,4096]{2,1,0:T(1,128)S(1)} all-gather(f32[1,1,4096]{2,1,0:T(1,128)S(1)} %get-tuple-element.234), channel_id=1, replica_groups=mesh['pb'=8,'ka'=32] {'pb'}, dimensions={0}, use_global_device_ids=true | all-gather | bytes 147456 | tf_op jit(solution)/shard_map/all_gather | solution.py:10
  289.5 69.1 %all-gather.3 = f32[131072]{0:T(1024)S(1)} all-gather(f32[4096]{0:T(1024)S(1)} %constant_dynamic-update-slice_fusion.3), channel_id=5, replica_groups=mesh['pb'=8,'ka'=32] {'ka'}, dimensions={0}, use_global_device_ids=true | all-gather | bytes 540672 | tf_op jit(solution)/shard_map/all_gather | solution.py:10
  358.8 40.7 %all-gather.2 = f32[131072]{0:T(1024)S(1)} all-gather(f32[4096]{0:T(1024)S(1)} %constant_dynamic-update-slice_fusion.2), channel_id=4, replica_groups=mesh['pb'=8,'ka'=32] {'ka'}, dimensions={0}, use_global_device_ids=true | all-gather | bytes 540672 | tf_op jit(solution)/shard_map/all_gather | solution.py:10
  399.7 41.9 %all-gather.1 = f32[131072]{0:T(1024)S(1)} all-gather(f32[4096]{0:T(1024)S(1)} %constant_dynamic-update-slice_fusion.1), channel_id=3, replica_groups=mesh['pb'=8,'ka'=32] {'ka'}, dimensions={0}, use_global_device_ids=true | all-gather | bytes 540672 | tf_op jit(solution)/shard_map/all_gather | solution.py:10
  441.7 41.1 %all-gather = f32[131072]{0:T(1024)S(1)} all-gather(f32[4096]{0:T(1024)S(1)} %constant_dynamic-update-slice_fusion), channel_id=2, replica_groups=mesh['pb'=8,'ka'=32] {'ka'}, dimensions={0}, use_global_device_ids=true | all-gather | bytes 540672 | tf_op jit(solution)/shard_map/all_gather | solution.py:10
  483.2 1.2 while.33
  484.7 4.9 while.32
  (274 shorter events, 8.0 us)
Async XLA Ops:
  7.2 43.1 %all-gather.13.cloned.1.call-start = ((), (), s32[]{:S(2)}) async-start(), calls=%async_computation.1 | async-start | bytes 1179648 | tf_op jit(solution)/shard_map/all_gather | solution.py:38
  7.9 101.4 %all-gather.11.cloned.1.call-start = ((), (), s32[]{:S(2)}) async-start(), calls=%async_computation | async-start | bytes 1081344 | tf_op jit(solution)/shard_map/all_gather | solution.py:37
  50.3 64.9 %copy-start = (bf16[4096,128]{1,0:T(8,128)(2,1)S(1)}, bf16[4096,128]{1,0:T(8,128)(2,1)}, u32[]{:S(2)}) copy-start(bf16[4096,128]{1,0:T(8,128)(2,1)} %all-gather.13.cloned.1.call-done) | copy-start | bytes 3145732
  109.3 5.9 %copy-start.1 = (bf16[4096,128]{1,0:T(8,128)(2,1)S(1)}, bf16[4096,128]{1,0:T(8,128)(2,1)}, u32[]{:S(2)}) copy-start(bf16[4096,128]{1,0:T(8,128)(2,1)} %all-gather.11.cloned.1.call-done) | copy-start | bytes 3145732
Sparse Core Ops, SparseCore 0:
  9.8 40.4 all-gather.12
  52.8 56.3 all-gather.10
where the time goes:
time: 498 us
  blocking collectives  280 us (56%)
  waiting for transfers between devices  102 us (20%)
  other arithmetic  70.7 us (14%)
  matrix products  24.7 us (5%)
  between operations  14.6 us (3%)
    all_gather x8, blocking collectives, joined(): pieces = jax.tree.map(lambda part: lax.all_gather(part, axis), value)  280 us
    reduce_sum x3, other arithmetic, on_device(): col_y = col_y * factor + jnp.sum(col_weights * query_y[:, None], axis=0)  67.1 us
    all_gather x1, waiting for transfers between devices, on_device(): queries = lax.all_gather(query_features, 'ka', axis=0, tiled=True)  59 us
    all_gather x1, waiting for transfers between devices, on_device(): keys = lax.all_gather(key_features, 'pb', axis=0, tiled=True)  41.3 us
    dot_general x8, matrix products, on_device(): lax.dot_general(rows, keys, (((1,), (1,)), ((), ())), preferred_element_t...  24.7 us
  transfers between devices with their start and end apart: 2, of which 2 were waited for; matrix products, arithmetic and copies ran while one was open for 0% of the time, Pallas kernels for 0%

commit v1 on v0

v1 whole, which is shorter than its diff:
```python
import functools
import math

import jax
import jax.numpy as jnp
from jax import lax
from jax.experimental import pallas as pl
from jax.experimental.pallas import tpu as pltpu
from jax.sharding import Mesh
from jax.sharding import PartitionSpec as P

FRAME_W = 480
CH = 128
NPIECE, PIECE = 8, 512
GROUP = 16
RUN = 32
TILES = 4
SCALE = math.log2(math.e) / math.sqrt(CH)
LOW, HIGH = 2.0**-90, 2.0**100
AXES = ("zl", "y", "zh", "x", "core")
SIZES = {"zl": 2, "y": 4, "zh": 4, "x": 4, "core": 2}
NT = (((1,), (1,)), ((), ()))


def nt_dot(a, b):
    return lax.dot_general(a, b, NT, preferred_element_type=jnp.float32)


def split2(v):
    high = v.astype(jnp.bfloat16)
    return high, (v - high.astype(jnp.float32)).astype(jnp.bfloat16)


def cell(n):
    y = ((n >> 5) * 4370) >> 16
    return (n - y * FRAME_W).astype(jnp.float32), y.astype(jnp.float32)


def iota(shape, axis):
    return lax.broadcasted_iota(jnp.int32, shape, axis)


def query_weights(sc, half):
    lane = iota((16, 256), 1)
    row = iota((16, 256), 0)
    on_sum = lane < 128
    lane = lane & 127
    s, g = lane >> 3, lane & 7
    shard = ((sc[2] * 4 + (s >> 2)) * 4 + sc[3]) * 8 + (s & 3) * 2 + half
    x, y = cell(shard * 128 + g * GROUP)
    value = jnp.where(
        row == 0, 1.0, jnp.where(row == 1, x + (GROUP - 256.0), jnp.where(row == 2, y, 0.0))
    )
    value = jnp.where(on_sum, value, jnp.where(row == 1, -1.0, 0.0))
    return value.astype(jnp.bfloat16)


def key_weights(sc, piece, half):
    x, y = cell(sc[8 + piece] + half * 256 + iota((8, 128), 0) * RUN)
    return x + (RUN - 256.0), y - 128.0


def unpack_rows(row_ref, values, half, stat):
    lane = iota((16, 128), 1) >> 3
    out = jnp.zeros((16, 128), jnp.float32)
    for t in range(GROUP):
        spread = jnp.broadcast_to(values[t : t + 1, :], (16, 128))
        turned = pltpu.roll(pltpu.roll(spread, 0, 1, stride=8, stride_axis=0), (t * 8 + 8) % 128, 1)
        out = jnp.where(lane == t, turned, out)
    for s in range(16):
        row_ref[half * 16 + s, stat : stat + 1, :] = out[15 - s : 16 - s, :]


def main_kernel(sc, qa, qb, *refs):
    k_refs = refs[:NPIECE]
    row_ref, col_ref, qf, qp, kk, acc, sums_ref, moments_ref, rm, km = refs[NPIECE:]

    def place(j, carry):
        slot = (j ^ sc[1]) * 128
        a = pl.multiple_of(sc[0] * 2048 + slot, 128)
        b = pl.multiple_of((1 - sc[0]) * 2048 + slot, 128)
        src = pl.ds(pl.multiple_of(j * 128, 128), 128)
        qf[pl.ds(a, 128), :] = qa[src, :].astype(jnp.float32)
        qf[pl.ds(b, 128), :] = qb[src, :].astype(jnp.float32)
        return carry

    lax.fori_loop(0, 16, place, 0)

    def tile(t, carry):
        for half in range(2):
            rows = [qf[pl.ds(half * 2048 + s * 128 + t, 8, stride=16), :] for s in range(16)]
            at = pl.multiple_of(half * 2048 + t * 128, 128)
            qp[pl.ds(at, 128), :] = jnp.concatenate(rows, 0).astype(jnp.bfloat16)
        return carry

    lax.fori_loop(0, GROUP, tile, 0, unroll=2)

    r, c = iota((256, 256), 0), iota((256, 256), 1)
    perm = jnp.where(c == (r & 7) * RUN + (r >> 3), 1.0, 0.0).astype(jnp.bfloat16)
    for piece in range(NPIECE):
        for half in range(2):
            at = piece * PIECE + half * 256
            kk[at : at + 256, :] = jnp.dot(
                perm, k_refs[piece][half * 256 : half * 256 + 256, :],
                preferred_element_type=jnp.float32,
            ).astype(jnp.bfloat16)

    def score(piece, half, lanes):
        at = pl.multiple_of(piece * PIECE + half * 256, 256)
        return nt_dot(kk[pl.ds(at, 256), :], qp[lanes, :]) * SCALE

    def stats(shifted):
        tiles = 1 if shifted else TILES
        acc[...] = jnp.zeros_like(acc)

        def one_piece(piece, carry):
            total = jnp.zeros((16, PIECE), jnp.float32)
            for side in range(2):
                sums_ref[...] = jnp.zeros_like(sums_ref)
                moments_ref[...] = jnp.zeros_like(moments_ref)

                def chunk(j, carry):
                    at = pl.multiple_of(side * 2048 + j * tiles * 128, tiles * 128)
                    lanes = pl.ds(at, tiles * 128)
                    for half in range(2):
                        s = score(piece, half, lanes)
                        if shifted:
                            top = km[pl.ds(pl.multiple_of(piece * PIECE + half * 256, 256), 256), :]
                            for_key = jnp.exp2(s - top)
                            for_query = jnp.exp2(s - rm[0:1, lanes])
                        else:
                            for_key = for_query = jnp.exp2(s)
                        sums, moments = [None] * tiles, [None] * tiles
                        for u in range(RUN):
                            rows = slice(half * 256 + u * 8, half * 256 + u * 8 + 8)
                            key_sum, key_moment = sums_ref[rows, :], moments_ref[rows, :]
                            for i in range(tiles):
                                part = (slice(u * 8, u * 8 + 8), slice(i * 128, i * 128 + 128))
                                e = for_query[part]
                                sums[i] = e if u == 0 else sums[i] + e
                                moments[i] = sums[i] if u == 0 else moments[i] + sums[i]
                                key_sum = key_sum + for_key[part]
                                key_moment = key_moment + key_sum
                            sums_ref[rows, :] = key_sum
                            moments_ref[rows, :] = key_moment
                        x, y = key_weights(sc, piece, half)
                        for i in range(tiles):
                            d = pl.ds(pl.multiple_of(at + i * 128, 128), 128)
                            acc[0, :, d] += sums[i]
                            acc[1, :, d] += sums[i] * x - moments[i]
                            acc[2, :, d] += sums[i] * y
                    return carry

                lax.fori_loop(0, GROUP // tiles, chunk, 0, unroll=1 if shifted else GROUP // tiles)
                w = query_weights(sc, side)
                for j in range(16):
                    half, run = j // 8, j % 8
                    there = pl.ds(half * 256 + run, RUN, stride=8)
                    v = jnp.concatenate([sums_ref[there, :], moments_ref[there, :]], 1)
                    hi, lo = split2(v)
                    if j % 4 == 0:
                        his, los = [], []
                    his.append(hi)
                    los.append(lo)
                    if j % 4 == 3:
                        a = (j // 4) * 128
                        got = nt_dot(w, jnp.concatenate(his, 0)) + nt_dot(w, jnp.concatenate(los, 0))
                        if side == 0:
                            col_ref[sc[16 + piece], 0:3, a : a + 128] = got[0:3]
                        else:
                            col_ref[sc[16 + piece], 0:3, a : a + 128] += got[0:3]
            if not shifted:
                col_ref[sc[16 + piece], 3:4, :] = jnp.zeros((1, PIECE), jnp.float32)
            return carry

        lax.fori_loop(0, NPIECE, one_piece, 0)
        for side in range(2):
            for stat in range(4):
                parts = []
                for t in range(GROUP):
                    d = slice(side * 2048 + t * 128, side * 2048 + t * 128 + 128)
                    if stat < 3:
                        parts.append(jnp.sum(acc[stat, :, d], axis=0, keepdims=True))
                    elif shifted:
                        parts.append(rm[0:1, d])
                if parts:
                    unpack_rows(row_ref, jnp.concatenate(parts, 0), side, stat)
                else:
                    row_ref[:, 3:4, :] = jnp.zeros((32, 1, 128), jnp.float32)

    stats(False)
    row_sums, col_sums = row_ref[:, 0, :], col_ref[:, 0, :]
    low = jnp.minimum(jnp.min(row_sums), jnp.min(col_sums))
    high = jnp.maximum(jnp.max(row_sums), jnp.max(col_sums))

    @pl.when(jnp.logical_not((low > LOW) & (high < HIGH)))
    def _():
        rm[...] = jnp.full_like(rm, -jnp.inf)

        def block(j, carry):
            piece, half = j >> 1, j & 1
            at = pl.multiple_of(j * 256, 256)

            def chunk(t, top):
                lanes = pl.ds(pl.multiple_of(t * 128, 128), 128)
                s = score(piece, half, lanes)
                rm[:, lanes] = jnp.maximum(rm[:, lanes], jnp.max(s.reshape(RUN, 8, 128), axis=0))
                return jnp.maximum(top, s)

            top = lax.fori_loop(
                0, 32, chunk, jnp.full((256, 128), -jnp.inf, jnp.float32)
            )
            top = jnp.max(top, axis=1, keepdims=True)
            hi, lo = split2(jnp.broadcast_to(top, (256, 128)))
            km[pl.ds(at, 256), :] = hi.astype(jnp.float32) + lo.astype(jnp.float32)
            return carry

        lax.fori_loop(0, 2 * NPIECE, block, 0)
        rm[...] = jnp.broadcast_to(jnp.max(rm[...], axis=0, keepdims=True), rm.shape)
        pick = jnp.where((iota((16, 128), 0) == 0) & (iota((16, 128), 1) == 0), 1.0, 0.0)
        pick = pick.astype(jnp.bfloat16)

        def tops(piece, carry):
            for j in range(16):
                half, run = j // 8, j % 8
                v = km[pl.ds(piece * PIECE + half * 256 + run, RUN, stride=8), :]
                hi, lo = split2(v)
                if j % 4 == 0:
                    his, los = [], []
                his.append(hi)
                los.append(lo)
                if j % 4 == 3:
                    a = (j // 4) * 128
                    got = nt_dot(pick, jnp.concatenate(his, 0)) + nt_dot(pick, jnp.concatenate(los, 0))
                    col_ref[sc[16 + piece], 3:4, a : a + 128] = got[0:1]
            return carry

        lax.fori_loop(0, NPIECE, tops, 0)
        stats(True)


def final_kernel(sc, rows, cols, f_ref, b_ref):
    def merged(parts, count):
        top = parts[0][3:4]
        for j in range(1, count):
            top = jnp.maximum(top, parts[j][3:4])
        total = None
        for j in range(count):
            v = parts[j][0:3] * jnp.exp2(parts[j][3:4] - top)
            total = v if total is None else total + v
        return total

    q = merged([rows[j] for j in range(32)], 32)
    n = sc[0] + (iota((1, 128), 1) & 7) * GROUP + (iota((1, 128), 1) >> 3)
    x, y = cell(n)
    fx = (q[1:2] / q[0:1] + (256.0 - x)) / FRAME_W
    fy = (q[2:3] / q[0:1] + (128.0 - y)) / FRAME_W
    r, c = iota((128, 128), 0), iota((128, 128), 1)
    order = jnp.where(c == (r & 7) * GROUP + (r >> 3), 1.0, 0.0).astype(jnp.bfloat16)
    flow = jnp.concatenate([fx, fy, jnp.zeros((6, 128), jnp.float32)], 0)
    out = jnp.zeros((8, 128), jnp.float32)
    for _ in range(3):
        part = flow.astype(jnp.bfloat16)
        out = out + jnp.dot(part, order, preferred_element_type=jnp.float32)
        flow = flow - part.astype(jnp.float32)
    f_ref[...] = out[0:2]
    k = merged([cols[j] for j in range(NPIECE)], NPIECE)
    x, y = cell(sc[1] + iota((1, PIECE), 1))
    b_ref[0:1, :] = (k[1:2] / k[0:1] + (256.0 - x)) / FRAME_W
    b_ref[1:2, :] = (k[2:3] / k[0:1] - y) / FRAME_W


def coords(i):
    out = {}
    for name in reversed(AXES):
        out[name] = i % SIZES[name]
        i //= SIZES[name]
    return out


def swap(value, **flips):
    def partner(i):
        at = coords(i)
        for name, flip in flips.items():
            at[name] ^= flip
        return functools.reduce(lambda a, name: a * SIZES[name] + at[name], AXES, 0)

    return lax.ppermute(value, AXES, [(i, partner(i)) for i in range(256)])


def ring(value, step):
    def partner(i):
        at = coords(i)
        z = (at["zh"] * 2 + at["zl"] + step) % 8
        at["zh"], at["zl"] = z // 2, z % 2
        return functools.reduce(lambda a, name: a * SIZES[name] + at[name], AXES, 0)

    return lax.ppermute(value, AXES, [(i, partner(i)) for i in range(256)])


def vmem(count):
    return [pl.BlockSpec(memory_space=pltpu.VMEM)] * count


def on_device(q, k):
    me = {name: lax.axis_index(name) for name in AXES}
    z = me["zh"] * 2 + me["zl"]
    pieces, offsets = [k], [0]
    up = down = k
    for step in range(1, 5):
        up = ring(up, 1)
        pieces.append(up)
        offsets.append(-step)
        if step < 4:
            down = ring(down, -1)
            pieces.append(down)
            offsets.append(step)
    a = jnp.concatenate([q] + [swap(q, x=j) for j in (1, 2, 3)])
    b = jnp.concatenate([a] + [swap(a, y=j) for j in (1, 2, 3)])
    other = swap(b, core=1)

    origin = [(z + off) % 8 for off in offsets]
    bases = [
        (((o // 2) * 8 + me["x"] * 2 + me["core"]) * 8 + (o % 2) * 4 + me["y"]) * PIECE
        for o in origin
    ]
    zero = jnp.int32(0)
    sc = jnp.stack(
        [me["core"], me["y"] * 4 + me["x"], me["zl"], me["zh"], zero, zero, zero, zero]
        + bases + origin
    ).astype(jnp.int32)
    smem = pl.BlockSpec(memory_space=pltpu.SMEM)
    rows, cols = pl.pallas_call(
        main_kernel,
        name="match",
        out_shape=[
            jax.ShapeDtypeStruct((32, 4, 128), jnp.float32),
            jax.ShapeDtypeStruct((8, 4, PIECE), jnp.float32),
        ],
        in_specs=[smem] + vmem(2 + NPIECE),
        out_specs=vmem(2),
        scratch_shapes=[
            pltpu.VMEM((4096, CH), jnp.float32),
            pltpu.VMEM((4096, CH), jnp.bfloat16),
            pltpu.VMEM((NPIECE * PIECE, CH), jnp.bfloat16),
            pltpu.VMEM((3, 8, 4096), jnp.float32),
            pltpu.VMEM((PIECE, 128), jnp.float32),
            pltpu.VMEM((PIECE, 128), jnp.float32),
            pltpu.VMEM((8, 4096), jnp.float32),
            pltpu.VMEM((NPIECE * PIECE, 128), jnp.float32),
        ],
        compiler_params=pltpu.CompilerParams(vmem_limit_bytes=48 * 2**20),
    )(sc, b, other, *pieces)
    rows = lax.all_to_all(rows, ("core", "y", "x"), 0, 0)
    cols = lax.all_to_all(cols, ("zh", "zl"), 0, 0)
    shard_q = ((me["zl"] * 4 + me["y"]) * 4 + me["zh"]) * 8 + me["x"] * 2 + me["core"]
    own = jnp.stack([shard_q * 128, bases[0]]).astype(jnp.int32)
    return pl.pallas_call(
        final_kernel,
        name="finish",
        out_shape=[
            jax.ShapeDtypeStruct((2, 128), jnp.float32),
            jax.ShapeDtypeStruct((2, PIECE), jnp.float32),
        ],
        in_specs=[smem] + vmem(2),
        out_specs=vmem(2),
    )(own, rows, cols)


def solution(mesh):
    fine = Mesh(mesh.devices.reshape(tuple(SIZES[name] for name in AXES)), AXES)
    query = P(AXES)
    key = P(("zh", "x", "core", "zl", "y"))
    return jax.shard_map(
        on_device,
        mesh=fine,
        in_specs=(query, key),
        out_specs=(P(None, AXES), P(None, ("zh", "x", "core", "zl", "y"))),
        check_vma=False,
    )
```

time: 498 us -> 270 us (0.54)
  blocking collectives: 280 us -> 13.7 us
  Pallas kernels: 0 us -> 198 us
  waiting for transfers between devices: 102 us -> 26 us
  other arithmetic: 70.7 us -> 0.62 us
  starting transfers between devices: 0.08 us -> 29.5 us
  matrix products: 24.7 us -> 0 us
  between operations: 14.6 us -> 0.69 us
    all_gather x8 -> x0, blocking collectives: 280 us -> none  [joined(): pieces = jax.tree.map(lambda part: lax.all_gather(part, axis), value)]
    pallas_call x0 -> x2, Pallas kernels: none -> 198 us  [the longest x1 196 us: on_device(): pl.pallas_call(main_kernel, name='match', out_shape=[jax.ShapeDtypeStruct...]
    all_gather x2 -> x0, waiting for transfers between devices: 100 us -> none  [the longest x1 59 us: on_device(): queries = lax.all_gather(query_features, 'ka', axis=0, tiled=True)]
    reduce_sum x3 -> x0, other arithmetic: 67.1 us -> none  [on_device(): col_y = col_y * factor + jnp.sum(col_weights * query_y[:, None], axis=0)]
    dot_general x8 -> x0, matrix products: 24.7 us -> none  [on_device(): lax.dot_general(rows, keys, (((1,), (1,)), ((), ())), preferred_element_t...]
    ppermute x0 -> x14, starting transfers between devices: none -> 23.9 us  [the longest x7 12.1 us: ring(): return lax.ppermute(value, AXES, [(i, partner(i)) for i in range(256)])]
    ppermute x0 -> x14, waiting for transfers between devices: none -> 19.3 us  [the longest x7 9.7 us: ring(): return lax.ppermute(value, AXES, [(i, partner(i)) for i in range(256)])]
    all_to_all x0 -> x1, blocking collectives: none -> 13.7 us  [on_device(): rows = lax.all_to_all(rows, ('core', 'y', 'x'), 0, 0)]
  transfers between devices with their start and end apart: 2 -> 15, of which waited for: 2 -> 9; matrix products, arithmetic and copies ran while one was open for 0% -> 1% of each run, Pallas kernels for 0% -> 0%
where the time goes in v1:
time: 270 us
  Pallas kernels  198 us (73%)
  starting transfers between devices  29.5 us (11%)
  waiting for transfers between devices  26 us (10%)
  blocking collectives  13.7 us (5%)
    pallas_call x1, Pallas kernels, on_device(): pl.pallas_call(main_kernel, name='match', out_shape=[jax.ShapeDtypeStruct...  196 us
    all_to_all x1, blocking collectives, on_device(): rows = lax.all_to_all(rows, ('core', 'y', 'x'), 0, 0)  13.7 us
    ppermute x7, starting transfers between devices, ring(): return lax.ppermute(value, AXES, [(i, partner(i)) for i in range(256)])  12.1 us
    ppermute x7, starting transfers between devices, swap(): return lax.ppermute(value, AXES, [(i, partner(i)) for i in range(256)])  11.8 us
    ppermute x7, waiting for transfers between devices, ring(): return lax.ppermute(value, AXES, [(i, partner(i)) for i in range(256)])  9.7 us
    ppermute x7, waiting for transfers between devices, swap(): return lax.ppermute(value, AXES, [(i, partner(i)) for i in range(256)])  9.57 us
    all_to_all x1, waiting for transfers between devices, on_device(): cols = lax.all_to_all(cols, ('zh', 'zl'), 0, 0)  6.71 us
    all_to_all x1, starting transfers between devices, on_device(): cols = lax.all_to_all(cols, ('zh', 'zl'), 0, 0)  5.56 us
  transfers between devices with their start and end apart: 15, of which 9 were waited for; matrix products, arithmetic and copies ran while one was open for 1% of the time, Pallas kernels for 0%

profile of v1, /device:TPU:1, one launch (start us, length us, event | category | flops | bytes accessed | tf_op | source)
XLA Modules:
  0.0 270.1 jit_solution(10144222895921401178)
XLA Ops:
  0.6 2.1 collective-permute-start
  2.8 2.5 collective-permute-start.1
  5.2 0.8 constant_dynamic-update-slice_fusion.3
  6.1 1.1 collective-permute-done.1
  7.3 2.1 collective-permute-done.2
  9.4 1.4 collective-permute-start.3
  10.8 2.6 collective-permute-start.4
  13.4 1.6 collective-permute-start.7
  15.1 2.1 collective-permute-done.4
  17.2 4.2 %collective-permute-done.5 = bf16[512,128]{1,0:T(8,128)(2,1)S(1)} collective-permute-done((bf16[512,128]{1,0:T(8,128)(2,1)S(1)}, bf16[512,128]{1,0:T(8,128)(2,1)S(1)}, u32[]{:S(2)}, u32[]{:S(2)}) %collective-permute-start.5) | collective-permute-done | bytes 131104 | tf_op jit(solution)/shard_map/ppermute | solution.py:288
  21.4 3.1 %collective-permute-start.6 = (bf16[2048,128]{1,0:T(8,128)(2,1)S(1)}, bf16[2048,128]{1,0:T(8,128)(2,1)S(1)}, u32[]{:S(2)}, u32[]{:S(2)}) collective-permute-start(bf16[2048,128]{1,0:T(8,128)(2,1)S(1)} %constant_dynamic-update-slice_fusion.4.qa), channel_id=1, source_target_pairs={{0,1},{1,0},{2,3},{3,2},{4,5},{5,4},{6,7},{7,6},{8,9},{9,8},{10,11... | collective-permute-start | bytes 1572872 | tf_op jit(solution)/shard_map/ppermute | solution.py:288
  24.6 3.7 %collective-permute-start.8 = (bf16[512,128]{1,0:T(8,128)(2,1)S(1)}, bf16[512,128]{1,0:T(8,128)(2,1)S(1)}, u32[]{:S(2)}, u32[]{:S(2)}) collective-permute-start(bf16[512,128]{1,0:T(8,128)(2,1)S(1)} %copy-done), channel_id=1, source_target_pairs={{0,152},{1,153},{2,154},{3,155},{4,156},{5,157},{6,158},{7,159},{8... | collective-permute-start | bytes 393224 | tf_op jit(solution)/shard_map/ppermute | solution.py:298
  28.2 2.8 %collective-permute-done.8.refs_2_ = bf16[512,128]{1,0:T(8,128)(2,1)S(1)} collective-permute-done((bf16[512,128]{1,0:T(8,128)(2,1)S(1)}, bf16[512,128]{1,0:T(8,128)(2,1)S(1)}, u32[]{:S(2)}, u32[]{:S(2)}) %collective-permute-start.8) | collective-permute-done | bytes 131104 | tf_op jit(solution)/shard_map/ppermute | solution.py:298
  31.1 3.4 %collective-permute-start.10 = (bf16[512,128]{1,0:T(8,128)(2,1)S(1)}, bf16[512,128]{1,0:T(8,128)(2,1)S(1)}, u32[]{:S(2)}, u32[]{:S(2)}) collective-permute-start(bf16[512,128]{1,0:T(8,128)(2,1)S(1)} %collective-permute-done.8.refs_2_), channel_id=1, source_target_pairs={{0,152},{1,153},{2,154},{3,155},{4,156},{5,157},{6,158},{7,159},{8... | collective-permute-start | bytes 393224 | tf_op jit(solution)/shard_map/ppermute | solution.py:298
  34.5 1.9 collective-permute-done.10.refs_4_
  36.4 3.4 %collective-permute-start.12 = (bf16[512,128]{1,0:T(8,128)(2,1)S(1)}, bf16[512,128]{1,0:T(8,128)(2,1)S(1)}, u32[]{:S(2)}, u32[]{:S(2)}) collective-permute-start(bf16[512,128]{1,0:T(8,128)(2,1)S(1)} %collective-permute-done.10.refs_4_), channel_id=1, source_target_pairs={{0,152},{1,153},{2,154},{3,155},{4,156},{5,157},{6,158},{7,159},{8... | collective-permute-start | bytes 393224 | tf_op jit(solution)/shard_map/ppermute | solution.py:298
  40.0 1.8 collective-permute-done.12.refs_6_
  41.8 3.1 %collective-permute-done.13.refs_7_ = bf16[512,128]{1,0:T(8,128)(2,1)S(1)} collective-permute-done((bf16[512,128]{1,0:T(8,128)(2,1)S(1)}, bf16[512,128]{1,0:T(8,128)(2,1)S(1)}, u32[]{:S(2)}, u32[]{:S(2)}) %collective-permute-start.13) | collective-permute-done | bytes 131104 | tf_op jit(solution)/shard_map/ppermute | solution.py:298
  44.9 196.3 %match.1 = (f32[32,4,128]{2,1,0:T(4,128)S(1)}, f32[8,4,512]{2,1,0:T(4,128)}) custom-call(s32[24]{0:T(128)S(1)} %stack.92.sc, bf16[2048,128]{1,0:T(8,128)(2,1)S(1)} %constant_dynamic-update-slice_fusion.4.qa, bf16[2048,128]{1,0:T(8,128)(2,1)S(1)} %collective-permute-done.6.qb, bf16[512,128]{1,0:T(8,128)(2,1)S(1)} %copy-done, ...), custom_call_target="tpu_custom_call" | custom-call | tf_op jit(solution)/shard_map/match/pallas_call | solution.py:333
  241.2 13.7 %all_to_all.10.rows = f32[32,4,128]{2,1,0:T(4,128)} all-to-all(f32[32,4,128]{2,1,0:T(4,128)S(1)} %get-tuple-element.4), channel_id=1, replica_groups=mesh['zl'=2,'y'=4,'zh'=4,'x'=4,'core'=2] {'core','y','x'}, dimensions={0} | all-to-all | bytes 131072 | tf_op jit(solution)/shard_map/all_to_all | solution.py:354
  254.9 5.6 %all-to-all-start.1 = ((f32[8,4,512]{2,1,0:T(4,128)}), f32[8,4,512]{2,1,0:T(4,128)S(1)}, u32[]{:S(2)}, u32[]{:S(2)}) async-start(f32[8,4,512]{2,1,0:T(4,128)} %get-tuple-element.5), calls=%async_computation.1 | async-start | bytes 131072 | tf_op jit(solution)/shard_map/all_to_all | solution.py:355
  261.1 6.7 %all-to-all-done.1.cols = f32[8,4,512]{2,1,0:T(4,128)S(1)} async-done(((f32[8,4,512]{2,1,0:T(4,128)}), f32[8,4,512]{2,1,0:T(4,128)S(1)}, u32[]{:S(2)}, u32[]{:S(2)}) %all-to-all-start.1) | async-done | bytes 65568 | tf_op jit(solution)/shard_map/all_to_all | solution.py:355
  267.8 0.6 copy-done.1
  268.4 1.7 finish.1
  (23 shorter events, 0.9 us)
Async XLA Ops:
  0.6 5.5 %collective-permute-start = (bf16[128,128]{1,0:T(8,128)(2,1)}, bf16[128,128]{1,0:T(8,128)(2,1)S(1)}, u32[]{:S(2)}, u32[]{:S(2)}) collective-permute-start(bf16[128,128]{1,0:T(8,128)(2,1)} %param.2), channel_id=1, source_target_pairs={{0,2},{1,3},{2,0},{3,1},{4,6},{5,7},{6,4},{7,5},{8,10},{9,11},{10,... | collective-permute-start | bytes 98312 | tf_op jit(solution)/shard_map/ppermute | solution.py:288
  2.8 4.5 %collective-permute-start.1 = (bf16[128,128]{1,0:T(8,128)(2,1)}, bf16[128,128]{1,0:T(8,128)(2,1)S(1)}, u32[]{:S(2)}, u32[]{:S(2)}) collective-permute-start(bf16[128,128]{1,0:T(8,128)(2,1)} %param.2), channel_id=1, source_target_pairs={{0,4},{1,5},{2,6},{3,7},{4,0},{5,1},{6,2},{7,3},{8,12},{9,13},{10,... | collective-permute-start | bytes 98312 | tf_op jit(solution)/shard_map/ppermute | solution.py:288
  5.2 4.2 %collective-permute-start.2 = (bf16[128,128]{1,0:T(8,128)(2,1)}, bf16[128,128]{1,0:T(8,128)(2,1)S(1)}, u32[]{:S(2)}, u32[]{:S(2)}) collective-permute-start(bf16[128,128]{1,0:T(8,128)(2,1)} %param.2), channel_id=1, source_target_pairs={{0,6},{1,7},{2,4},{3,5},{4,2},{5,3},{6,0},{7,1},{8,14},{9,15},{10,... | collective-permute-start | bytes 98312 | tf_op jit(solution)/shard_map/ppermute | solution.py:288
  6.1 7.3 %copy-start = (bf16[512,128]{1,0:T(8,128)(2,1)S(1)}, bf16[512,128]{1,0:T(8,128)(2,1)}, u32[]{:S(2)}) copy-start(bf16[512,128]{1,0:T(8,128)(2,1)} %refs_0_.1) | copy-start | bytes 393220
  9.4 5.7 %collective-permute-start.3 = (bf16[512,128]{1,0:T(8,128)(2,1)S(1)}, bf16[512,128]{1,0:T(8,128)(2,1)S(1)}, u32[]{:S(2)}, u32[]{:S(2)}) collective-permute-start(bf16[512,128]{1,0:T(8,128)(2,1)S(1)} %get-tuple-element.6), channel_id=1, source_target_pairs={{0,32},{1,33},{2,34},{3,35},{4,36},{5,37},{6,38},{7,39},{8,40},{9,... | collective-permute-start | bytes 393224 | tf_op jit(solution)/shard_map/ppermute | solution.py:288
  10.8 6.4 %collective-permute-start.4 = (bf16[512,128]{1,0:T(8,128)(2,1)S(1)}, bf16[512,128]{1,0:T(8,128)(2,1)S(1)}, u32[]{:S(2)}, u32[]{:S(2)}) collective-permute-start(bf16[512,128]{1,0:T(8,128)(2,1)S(1)} %get-tuple-element.6), channel_id=1, source_target_pairs={{0,64},{1,65},{2,66},{3,67},{4,68},{5,69},{6,70},{7,71},{8,72},{9,... | collective-permute-start | bytes 393224 | tf_op jit(solution)/shard_map/ppermute | solution.py:288
  13.4 14.8 %collective-permute-start.7 = (bf16[512,128]{1,0:T(8,128)(2,1)S(1)}, bf16[512,128]{1,0:T(8,128)(2,1)S(1)}, u32[]{:S(2)}, u32[]{:S(2)}) collective-permute-start(bf16[512,128]{1,0:T(8,128)(2,1)S(1)} %copy-done), channel_id=1, source_target_pairs={{0,128},{1,129},{2,130},{3,131},{4,132},{5,133},{6,134},{7,135},{8... | collective-permute-start | bytes 393224 | tf_op jit(solution)/shard_map/ppermute | solution.py:298
  15.1 6.4 %collective-permute-start.5 = (bf16[512,128]{1,0:T(8,128)(2,1)S(1)}, bf16[512,128]{1,0:T(8,128)(2,1)S(1)}, u32[]{:S(2)}, u32[]{:S(2)}) collective-permute-start(bf16[512,128]{1,0:T(8,128)(2,1)S(1)} %get-tuple-element.6), channel_id=1, source_target_pairs={{0,96},{1,97},{2,98},{3,99},{4,100},{5,101},{6,102},{7,103},{8,104... | collective-permute-start | bytes 393224 | tf_op jit(solution)/shard_map/ppermute | solution.py:288
  21.4 23.5 %collective-permute-start.6 = (bf16[2048,128]{1,0:T(8,128)(2,1)S(1)}, bf16[2048,128]{1,0:T(8,128)(2,1)S(1)}, u32[]{:S(2)}, u32[]{:S(2)}) collective-permute-start(bf16[2048,128]{1,0:T(8,128)(2,1)S(1)} %constant_dynamic-update-slice_fusion.4.qa), channel_id=1, source_target_pairs={{0,1},{1,0},{2,3},{3,2},{4,5},{5,4},{6,7},{7,6},{8,9},{9,8},{10,11... | collective-permute-start | bytes 1572872 | tf_op jit(solution)/shard_map/ppermute | solution.py:288
  24.6 6.5 %collective-permute-start.8 = (bf16[512,128]{1,0:T(8,128)(2,1)S(1)}, bf16[512,128]{1,0:T(8,128)(2,1)S(1)}, u32[]{:S(2)}, u32[]{:S(2)}) collective-permute-start(bf16[512,128]{1,0:T(8,128)(2,1)S(1)} %copy-done), channel_id=1, source_target_pairs={{0,152},{1,153},{2,154},{3,155},{4,156},{5,157},{6,158},{7,159},{8... | collective-permute-start | bytes 393224 | tf_op jit(solution)/shard_map/ppermute | solution.py:298
  28.2 6.3 %collective-permute-start.9 = (bf16[512,128]{1,0:T(8,128)(2,1)S(1)}, bf16[512,128]{1,0:T(8,128)(2,1)S(1)}, u32[]{:S(2)}, u32[]{:S(2)}) collective-permute-start(bf16[512,128]{1,0:T(8,128)(2,1)S(1)} %collective-permute-done.7.refs_1_), channel_id=1, source_target_pairs={{0,128},{1,129},{2,130},{3,131},{4,132},{5,133},{6,134},{7,135},{8... | collective-permute-start | bytes 393224 | tf_op jit(solution)/shard_map/ppermute | solution.py:298
  31.1 5.4 %collective-permute-start.10 = (bf16[512,128]{1,0:T(8,128)(2,1)S(1)}, bf16[512,128]{1,0:T(8,128)(2,1)S(1)}, u32[]{:S(2)}, u32[]{:S(2)}) collective-permute-start(bf16[512,128]{1,0:T(8,128)(2,1)S(1)} %collective-permute-done.8.refs_2_), channel_id=1, source_target_pairs={{0,152},{1,153},{2,154},{3,155},{4,156},{5,157},{6,158},{7,159},{8... | collective-permute-start | bytes 393224 | tf_op jit(solution)/shard_map/ppermute | solution.py:298
  34.5 5.4 %collective-permute-start.11 = (bf16[512,128]{1,0:T(8,128)(2,1)S(1)}, bf16[512,128]{1,0:T(8,128)(2,1)S(1)}, u32[]{:S(2)}, u32[]{:S(2)}) collective-permute-start(bf16[512,128]{1,0:T(8,128)(2,1)S(1)} %collective-permute-done.9.refs_3_), channel_id=1, source_target_pairs={{0,128},{1,129},{2,130},{3,131},{4,132},{5,133},{6,134},{7,135},{8... | collective-permute-start | bytes 393224 | tf_op jit(solution)/shard_map/ppermute | solution.py:298
  36.4 5.4 %collective-permute-start.12 = (bf16[512,128]{1,0:T(8,128)(2,1)S(1)}, bf16[512,128]{1,0:T(8,128)(2,1)S(1)}, u32[]{:S(2)}, u32[]{:S(2)}) collective-permute-start(bf16[512,128]{1,0:T(8,128)(2,1)S(1)} %collective-permute-done.10.refs_4_), channel_id=1, source_target_pairs={{0,152},{1,153},{2,154},{3,155},{4,156},{5,157},{6,158},{7,159},{8... | collective-permute-start | bytes 393224 | tf_op jit(solution)/shard_map/ppermute | solution.py:298
  39.9 5.0 %collective-permute-start.13 = (bf16[512,128]{1,0:T(8,128)(2,1)S(1)}, bf16[512,128]{1,0:T(8,128)(2,1)S(1)}, u32[]{:S(2)}, u32[]{:S(2)}) collective-permute-start(bf16[512,128]{1,0:T(8,128)(2,1)S(1)} %collective-permute-done.11.refs_5_), channel_id=1, source_target_pairs={{0,128},{1,129},{2,130},{3,131},{4,132},{5,133},{6,134},{7,135},{8... | collective-permute-start | bytes 393224 | tf_op jit(solution)/shard_map/ppermute | solution.py:298
  254.9 12.9 %all-to-all-start.1 = ((f32[8,4,512]{2,1,0:T(4,128)}), f32[8,4,512]{2,1,0:T(4,128)S(1)}, u32[]{:S(2)}, u32[]{:S(2)}) async-start(f32[8,4,512]{2,1,0:T(4,128)} %get-tuple-element.5), calls=%async_computation.1 | async-start | bytes 131072 | tf_op jit(solution)/shard_map/all_to_all | solution.py:355
  267.8 0.6 copy-start.1

commit v2 on v0

v2 whole, which is shorter than its diff:
```python
import functools
import math

import jax
import jax.numpy as jnp
from jax import lax
from jax.experimental import pallas as pl
from jax.experimental.pallas import tpu as pltpu
from jax.sharding import Mesh
from jax.sharding import PartitionSpec as P

FRAME_W = 480
CH = 128
BAND = 4096
PIECE = 512
RUN = 32
ORDER = (0, 1, 3, 2)
TILES = 4
SCALE = math.log2(math.e) / math.sqrt(CH)
LOW, HIGH = 2.0**-90, 2.0**100
AXES = ("zl", "y", "zh", "x", "core")
SIZES = {"zl": 2, "y": 4, "zh": 4, "x": 4, "core": 2}
NT = (((1,), (1,)), ((), ()))
CORE, X, Y, Z, PIECE_Z = 0, 1, 2, 3, 4


def nt_dot(a, b):
    return lax.dot_general(a, b, NT, preferred_element_type=jnp.float32)


def split2(v):
    high = v.astype(jnp.bfloat16)
    return high, (v - high.astype(jnp.float32)).astype(jnp.bfloat16)


def cell(n):
    y = ((n >> 5) * 4370) >> 16
    return (n - y * FRAME_W).astype(jnp.float32), y.astype(jnp.float32)


def iota(shape, axis):
    return lax.broadcasted_iota(jnp.int32, shape, axis)


def key_base(z, y, x, core):
    return ((((z >> 1) * 4 + x) * 2 + core) * 8 + (z & 1) * 4 + y) * 512


def query_base(z, y, x, core):
    return ((((z & 1) * 4 + y) * 4 + (z >> 1)) * 8 + x * 2 + core) * 128


def key_weights(sc):
    lane = iota((16, 256), 1)
    row = iota((16, 256), 0)
    on_sum = lane < 128
    s, g = (lane >> 4) & 7, lane & 15
    x, y = cell(key_base(sc[Z], sc[Y], s & 3, s >> 2) + g * RUN)
    x, y = x + (RUN - 256.0), y - 128.0
    value = jnp.where(row == 0, 1.0, jnp.where(row == 1, x, jnp.where(row == 2, y, 0.0)))
    value = jnp.where(on_sum, value, jnp.where(row == 1, -1.0, 0.0))
    return value.astype(jnp.bfloat16)


def query_weights(sc, z, half):
    r = iota((8, 128), 0)
    slot = jnp.where(r < 4, ORDER[2 * half], ORDER[2 * half + 1])
    x, y = cell(query_base(z, sc[Y] ^ slot, sc[X], sc[CORE]) + (r & 3) * RUN)
    return x + (RUN - 256.0), y


def run_order():
    r, c = iota((256, 256), 0), iota((256, 256), 1)
    return jnp.where(c == (r & 7) * RUN + (r >> 3), 1.0, 0.0).astype(jnp.bfloat16)


def set_keys(sc, ka, kb, kf, kp):
    for j in range(4):
        slot = sc[X] ^ ORDER[j]
        for core, ref in ((sc[CORE], ka), (1 - sc[CORE], kb)):
            at = pl.multiple_of((core * 4 + slot) * 512, 512)
            kf[pl.ds(at, 512), :] = ref[j * 512 : j * 512 + 512, :].astype(jnp.float32)

    def tile(t, carry):
        rows = [kf[pl.ds(s * 512 + t, 16, stride=RUN), :] for s in range(8)]
        at = pl.multiple_of(t * 128, 128)
        kp[pl.ds(at, 128), :] = jnp.concatenate(rows, 0).astype(jnp.bfloat16)
        return carry

    lax.fori_loop(0, RUN, tile, 0, unroll=4)


def set_queries(ref, qp):
    perm = run_order()
    for half in range(2):
        rows = slice(half * 256, half * 256 + 256)
        qp[rows, :] = jnp.dot(perm, ref[rows, :], preferred_element_type=jnp.float32).astype(
            jnp.bfloat16
        )


def in_order(refs, part):
    got = []
    for run in range(4 * part, 4 * part + 4):
        there = pl.ds((run // 8) * 256 + run % 8, RUN, stride=8)
        got.append(jnp.concatenate([ref[there, :] for ref in refs], 1))
    return split2(jnp.concatenate(got, 0))


def one_piece(sc, z, qp, kp, acc, sums_ref, moments_ref, store, tops=None):
    tiles = TILES if tops is None else 1
    sums_ref[...] = jnp.zeros_like(sums_ref)
    moments_ref[...] = jnp.zeros_like(moments_ref)
    weights = [query_weights(sc, z, half) for half in range(2)]

    def chunk(j, carry):
        at = pl.multiple_of(j * tiles * 128, tiles * 128)
        lanes = pl.ds(at, tiles * 128)
        for half in range(2):
            s = nt_dot(qp[half * 256 : half * 256 + 256, :], kp[lanes, :]) * SCALE
            if tops is None:
                for_query = for_key = jnp.exp2(s)
            else:
                for_query = jnp.exp2(s - tops[0][half * 256 : half * 256 + 256, :])
                for_key = jnp.exp2(s - tops[1][0:1, lanes])
            sums, moments = [None] * tiles, [None] * tiles
            for u in range(RUN):
                rows = slice(half * 256 + u * 8, half * 256 + u * 8 + 8)
                own_sum, own_moment = sums_ref[rows, :], moments_ref[rows, :]
                for i in range(tiles):
                    part = (slice(u * 8, u * 8 + 8), slice(i * 128, i * 128 + 128))
                    e = for_key[part]
                    sums[i] = e if u == 0 else sums[i] + e
                    moments[i] = sums[i] if u == 0 else moments[i] + sums[i]
                    own_sum = own_sum + for_query[part]
                    own_moment = own_moment + own_sum
                sums_ref[rows, :] = own_sum
                moments_ref[rows, :] = own_moment
            x, y = weights[half]
            for i in range(tiles):
                d = pl.ds(pl.multiple_of(at + i * 128, 128), 128)
                acc[0, :, d] += sums[i]
                acc[1, :, d] += sums[i] * x - moments[i]
                acc[2, :, d] += sums[i] * y
        return carry

    count = BAND // 128 // tiles
    lax.fori_loop(0, count, chunk, 0, unroll=4 if tops is None else 1)
    w = key_weights(sc)
    for slot in range(4):
        hi, lo = in_order((sums_ref, moments_ref), slot)
        got = nt_dot(w, hi) + nt_dot(w, lo)
        store(slot, slice(0, 3), got[0:3])


def spread_keys(col_ref, acc, top=None):
    lane = iota((8, 128), 1) >> 4
    for stat in range(4):
        if stat == 3 and top is None:
            col_ref[:, 3:4, :] = jnp.zeros((8, 1, 512), jnp.float32)
            continue
        for block in range(4):
            out = jnp.zeros((8, 128), jnp.float32)
            for t in range(8):
                d = slice((block * 8 + t) * 128, (block * 8 + t) * 128 + 128)
                value = top[0:1, d] if stat == 3 else jnp.sum(acc[stat, :, d], 0, keepdims=True)
                value = pltpu.roll(jnp.broadcast_to(value, (8, 128)), 0, 1, stride=16, stride_axis=0)
                out = jnp.where(lane == t, pltpu.roll(value, (t * 16 + 16) % 128, 1), out)
            for s in range(8):
                lanes = slice(block * 128, block * 128 + 128)
                col_ref[s, stat : stat + 1, lanes] = out[7 - s : 8 - s, :]


def first_kernel(sc, ka, kb, q, kp, acc, rows, kf, qp, sums_ref, moments_ref):
    set_keys(sc, ka, kb, kf, kp)
    acc[...] = jnp.zeros_like(acc)
    set_queries(q, qp)

    def store(slot, stats, value):
        rows[0, slot, stats, :] = value

    one_piece(sc, sc[PIECE_Z], qp, kp, acc, sums_ref, moments_ref, store)


def more_kernel(first, sc, kp, old, *refs):
    count = (len(refs) - 5) // 1
    qs, (acc, rows, qp, sums_ref, moments_ref) = refs[:count], refs[count:]
    acc[...] = old[...]
    for i, q in enumerate(qs):
        set_queries(q, qp)

        def store(slot, stats, value, i=i):
            rows[i, slot, stats, :] = value

        one_piece(sc, sc[PIECE_Z + first + i], qp, kp, acc, sums_ref, moments_ref, store)


def last_kernel(sc, kp, old, q, r0, r1, r2, r3, *refs):
    pieces, refs = refs[:8], refs[8:]
    row_ref, col_ref, acc, qp, sums_ref, moments_ref, rm, km, raw, sem = refs
    acc[...] = old[...]
    set_queries(q, qp)

    def place(piece, slot):
        return sc[PIECE_Z + piece] * 4 + (sc[Y] ^ ORDER[slot])

    def store(piece, slot, stats, value):
        row_ref[place(piece, slot), stats, :] = value

    one_piece(
        sc, sc[PIECE_Z + 7], qp, kp, acc, sums_ref, moments_ref, functools.partial(store, 7)
    )
    piece = 0
    for ref in (r0, r1, r2, r3):
        for i in range(ref.shape[0]):
            for slot in range(4):
                store(piece, slot, slice(0, 3), ref[i, slot, 0:3, :])
            piece += 1
    row_ref[:, 3:4, :] = jnp.zeros((32, 1, 128), jnp.float32)
    spread_keys(col_ref, acc)
    row_sums, col_sums = row_ref[:, 0, :], col_ref[:, 0, :]
    low = jnp.minimum(jnp.min(row_sums), jnp.min(col_sums))
    high = jnp.maximum(jnp.max(row_sums), jnp.max(col_sums))

    @pl.when(jnp.logical_not((low > LOW) & (high < HIGH)))
    def _():
        acc[...] = jnp.zeros_like(acc)
        km[...] = jnp.full_like(km, -jnp.inf)
        pick = jnp.where((iota((16, 128), 0) == 0) & (iota((16, 128), 1) == 0), 1.0, 0.0)
        pick = pick.astype(jnp.bfloat16)

        def fetch(piece):
            copy = pltpu.make_async_copy(pieces[piece], raw, sem)
            copy.start()
            copy.wait()
            set_queries(raw, qp)

        def block_top(half, t):
            lanes = pl.ds(pl.multiple_of(t * 128, 128), 128)
            s = nt_dot(qp[half * 256 : half * 256 + 256, :], kp[lanes, :]) * SCALE
            return lanes, s

        for piece in range(8):
            fetch(piece)

            def chunk(t, carry):
                for half in range(2):
                    lanes, s = block_top(half, t)
                    km[:, lanes] = jnp.maximum(km[:, lanes], jnp.max(s.reshape(RUN, 8, 128), 0))
                return carry

            lax.fori_loop(0, BAND // 128, chunk, 0)
        km[...] = jnp.broadcast_to(jnp.max(km[...], 0, keepdims=True), km.shape)
        for piece in range(8):
            fetch(piece)
            for half in range(2):

                def chunk(t, top, half=half):
                    return jnp.maximum(top, block_top(half, t)[1])

                top = jnp.full((256, 128), -jnp.inf, jnp.float32)
                top = lax.fori_loop(0, BAND // 128, chunk, top)
                hi, lo = split2(jnp.broadcast_to(jnp.max(top, 1, keepdims=True), (256, 128)))
                rm[half * 256 : half * 256 + 256, :] = hi.astype(jnp.float32) + lo.astype(
                    jnp.float32
                )
            for slot in range(4):
                hi, lo = in_order((rm,), slot)
                store(piece, slot, slice(3, 4), (nt_dot(pick, hi) + nt_dot(pick, lo))[0:1])
            one_piece(
                sc, sc[PIECE_Z + piece], qp, kp, acc, sums_ref, moments_ref,
                functools.partial(store, piece), (rm, km),
            )
        spread_keys(col_ref, acc, km)


def final_kernel(sc, rows, cols, f_ref, b_ref):
    def merged(parts):
        top = parts[0][3:4]
        for part in parts[1:]:
            top = jnp.maximum(top, part[3:4])
        return sum(part[0:3] * jnp.exp2(part[3:4] - top) for part in parts)

    q = merged([rows[j] for j in range(32)])
    x, y = cell(query_base(sc[Z], sc[Y], sc[X], sc[CORE]) + iota((1, 128), 1))
    f_ref[0:1, :] = (q[1:2] / q[0:1] + (256.0 - x)) / FRAME_W
    f_ref[1:2, :] = (q[2:3] / q[0:1] + (128.0 - y)) / FRAME_W
    k = merged([cols[j] for j in range(8)])
    lane = iota((1, 512), 1)
    x, y = cell(key_base(sc[Z], sc[Y], sc[X], sc[CORE]) + (lane & 15) * RUN + (lane >> 4))
    bx = (k[1:2] / k[0:1] + (256.0 - x)) / FRAME_W
    by = (k[2:3] / k[0:1] - y) / FRAME_W
    r, c = iota((512, 512), 0), iota((512, 512), 1)
    order = jnp.where(c == (r & 15) * RUN + (r >> 4), 1.0, 0.0).astype(jnp.bfloat16)
    flow = jnp.concatenate([bx, by, jnp.zeros((6, 512), jnp.float32)], 0)
    parts = []
    for _ in range(3):
        parts.append(flow.astype(jnp.bfloat16))
        flow = flow - parts[-1].astype(jnp.float32)
    out = jnp.dot(jnp.concatenate(parts, 0), order, preferred_element_type=jnp.float32)
    b_ref[...] = out[0:2] + out[8:10] + out[16:18]


def coords(i):
    out = {}
    for name in reversed(AXES):
        out[name] = i % SIZES[name]
        i //= SIZES[name]
    return out


def index(at):
    return functools.reduce(lambda a, name: a * SIZES[name] + at[name], AXES, 0)


def swap(value, **flips):
    def partner(i):
        at = coords(i)
        for name, flip in flips.items():
            at[name] ^= flip
        return index(at)

    return lax.ppermute(value, AXES, [(i, partner(i)) for i in range(256)])


def ring(value, step):
    def partner(i):
        at = coords(i)
        z = (at["zh"] * 2 + at["zl"] + step) % 8
        at["zh"], at["zl"] = z // 2, z % 2
        return index(at)

    return lax.ppermute(value, AXES, [(i, partner(i)) for i in range(256)])


SMEM = pl.BlockSpec(memory_space=pltpu.SMEM)
VMEM = pl.BlockSpec(memory_space=pltpu.VMEM)
ANY = pl.BlockSpec(memory_space=pl.ANY)


def f32(*shape):
    return jax.ShapeDtypeStruct(shape, jnp.float32)


def call(kernel, name, args, in_specs, out_shape, scratch, pieces, alias=None):
    return pl.pallas_call(
        kernel,
        name=name,
        out_shape=out_shape,
        in_specs=in_specs,
        out_specs=[VMEM] * len(out_shape),
        scratch_shapes=scratch,
        input_output_aliases=alias or {},
        cost_estimate=pl.CostEstimate(
            flops=pieces * 2 * PIECE * BAND * 256, bytes_accessed=2**21, transcendentals=pieces * PIECE * BAND
        ),
        compiler_params=pltpu.CompilerParams(vmem_limit_bytes=40 * 2**20),
    )(*args)


def on_device(q, k):
    me = {name: lax.axis_index(name) for name in AXES}
    z = me["zh"] * 2 + me["zl"]
    ka = jnp.concatenate([k] + [swap(k, x=j) for j in ORDER[1:]])
    own = jnp.concatenate([q] + [swap(q, y=j) for j in ORDER[1:]])
    kb = swap(ka, core=1)
    z_of = [(z + off) % 8 for off in (0, -1, 1, -2, 2, -3, 3, -4)]
    sc = jnp.stack([me["core"], me["x"], me["y"], z] + z_of).astype(jnp.int32)

    half_sums = [pltpu.VMEM((PIECE, 128), jnp.float32)] * 2
    piece_rows = pltpu.VMEM((PIECE, CH), jnp.bfloat16)
    pieces = [own, ring(own, 1), ring(own, -1)]
    kp, acc, r0 = call(
        first_kernel, "first", (sc, ka, kb, own), [SMEM, VMEM, VMEM, VMEM],
        [jax.ShapeDtypeStruct((BAND, CH), jnp.bfloat16), f32(3, 8, BAND), f32(1, 4, 4, 128)],
        [pltpu.VMEM((BAND, CH), jnp.float32), piece_rows] + half_sums, 1,
    )
    parts = [r0]
    for first in (1, 3, 5):
        up, down, acc = lax.optimization_barrier((pieces[first], pieces[first + 1], acc))
        pieces += [ring(up, 1), ring(down, -1)] if first < 5 else [ring(up, 1)]
        acc, got = call(
            functools.partial(more_kernel, first), f"more{first}",
            (sc, kp, acc, up, down), [SMEM] + [VMEM] * 4,
            [f32(3, 8, BAND), f32(2, 4, 4, 128)], [piece_rows] + half_sums, 2,
        )
        parts.append(got)
    rows, cols = call(
        last_kernel, "last", (sc, kp, acc, pieces[7], *parts, *pieces),
        [SMEM] + [VMEM] * 7 + [ANY] * 8, [f32(32, 4, 128), f32(8, 4, 512)],
        [pltpu.VMEM((3, 8, BAND), jnp.float32), piece_rows] + half_sums
        + [pltpu.VMEM((PIECE, 128), jnp.float32), pltpu.VMEM((8, BAND), jnp.float32),
           piece_rows, pltpu.SemaphoreType.DMA], 1,
    )
    rows = lax.all_to_all(rows, ("zh", "zl", "y"), 0, 0)
    cols = lax.all_to_all(cols, ("core", "x"), 0, 0)
    return call(
        final_kernel, "finish", (sc, rows, cols), [SMEM, VMEM, VMEM], [f32(2, 128), f32(2, 512)], [], 0
    )


def solution(mesh):
    fine = Mesh(mesh.devices.reshape(tuple(SIZES[name] for name in AXES)), AXES)
    key = ("zh", "x", "core", "zl", "y")
    return jax.shard_map(
        on_device,
        mesh=fine,
        in_specs=(P(AXES), P(key)),
        out_specs=(P(None, AXES), P(None, key)),
        check_vma=False,
    )
```

time: 498 us -> 304 us (0.61)
  blocking collectives: 280 us -> 27.4 us
  Pallas kernels: 0 us -> 245 us
  waiting for transfers between devices: 102 us -> 8.35 us
  other arithmetic: 70.7 us -> 0 us
  matrix products: 24.7 us -> 0 us
  starting transfers between devices: 0.08 us -> 20.8 us
  between operations: 14.6 us -> 0.71 us
    all_gather x8 -> x0, blocking collectives: 280 us -> none  [joined(): pieces = jax.tree.map(lambda part: lax.all_gather(part, axis), value)]
    pallas_call x0 -> x6, Pallas kernels: none -> 245 us  [call(): pl.pallas_call(kernel, name=name, out_shape=out_shape, in_specs=in_specs,...]
    all_gather x2 -> x0, waiting for transfers between devices: 100 us -> none  [the longest x1 59 us: on_device(): queries = lax.all_gather(query_features, 'ka', axis=0, tiled=True)]
    reduce_sum x3 -> x0, other arithmetic: 67.1 us -> none  [on_device(): col_y = col_y * factor + jnp.sum(col_weights * query_y[:, None], axis=0)]
    all_to_all x0 -> x2, blocking collectives: none -> 27.4 us  [the longest x1 15.3 us: on_device(): rows = lax.all_to_all(rows, ('zh', 'zl', 'y'), 0, 0)]
    dot_general x8 -> x0, matrix products: 24.7 us -> none  [on_device(): lax.dot_general(rows, keys, (((1,), (1,)), ((), ())), preferred_element_t...]
    ppermute x0 -> x14, starting transfers between devices: none -> 20.8 us  [the longest x7 10.5 us: swap(): return lax.ppermute(value, AXES, [(i, partner(i)) for i in range(256)])]
    ppermute x0 -> x14, waiting for transfers between devices: none -> 8.35 us  [the longest x7 8.33 us: swap(): return lax.ppermute(value, AXES, [(i, partner(i)) for i in range(256)])]
  transfers between devices with their start and end apart: 2 -> 14, of which waited for: 2 -> 4; matrix products, arithmetic and copies ran while one was open for 0% -> 0% of each run, Pallas kernels for 0% -> 8%
where the time goes in v2:
time: 304 us
  Pallas kernels  245 us (81%)
  blocking collectives  27.4 us (9%)
  starting transfers between devices  20.8 us (7%)
  waiting for transfers between devices  8.35 us (3%)
    pallas_call x6, Pallas kernels, call(): pl.pallas_call(kernel, name=name, out_shape=out_shape, in_specs=in_specs,...  245 us
    all_to_all x1, blocking collectives, on_device(): rows = lax.all_to_all(rows, ('zh', 'zl', 'y'), 0, 0)  15.3 us
    all_to_all x1, blocking collectives, on_device(): cols = lax.all_to_all(cols, ('core', 'x'), 0, 0)  12.1 us
    ppermute x7, starting transfers between devices, swap(): return lax.ppermute(value, AXES, [(i, partner(i)) for i in range(256)])  10.5 us
    ppermute x7, starting transfers between devices, ring(): return lax.ppermute(value, AXES, [(i, partner(i)) for i in range(256)])  10.3 us
    ppermute x7, waiting for transfers between devices, swap(): return lax.ppermute(value, AXES, [(i, partner(i)) for i in range(256)])  8.33 us
  transfers between devices with their start and end apart: 14, of which 4 were waited for; matrix products, arithmetic and copies ran while one was open for 0% of the time, Pallas kernels for 8%

profile of v2, /device:TPU:1, one launch (start us, length us, event | category | flops | bytes accessed | tf_op | source)
XLA Modules:
  0.0 303.8 jit_solution(296029551057635150)
XLA Ops:
  0.6 2.1 collective-permute-start
  2.8 1.8 collective-permute-start.1
  4.6 0.6 collective-permute-start.2
  5.2 0.9 constant_dynamic-update-slice_fusion.3
  6.2 1.8 collective-permute-done.1
  8.0 3.0 collective-permute-done.2
  11.1 2.4 collective-permute-start.3
  13.4 1.0 collective-permute-start.4
  14.4 1.9 collective-permute-start.5
  16.3 0.7 collective-permute-start.6
  17.0 1.3 collective-permute-done.5
  18.4 2.2 collective-permute-done.6
  20.6 1.6 collective-permute-start.7
  22.2 4.0 %collective-permute-start.8 = (bf16[512,128]{1,0:T(8,128)(2,1)S(1)}, bf16[512,128]{1,0:T(8,128)(2,1)S(1)}, u32[]{:S(2)}, u32[]{:S(2)}) collective-permute-start(bf16[512,128]{1,0:T(8,128)(2,1)S(1)} %constant_dynamic-update-slice_fusion.4.q.refs_0_), channel_id=1, source_target_pairs={{0,152},{1,153},{2,154},{3,155},{4,156},{5,157},{6,158},{7,159},{8... | collective-permute-start | bytes 393224 | tf_op jit(solution)/shard_map/ppermute | solution.py:333
  26.3 5.2 %first.1 = (bf16[4096,128]{1,0:T(8,128)(2,1)S(1)}, f32[3,8,4096]{2,1,0:T(8,128)S(1)}, f32[1,4,4,128]{3,2,1,0:T(4,128)S(1)}) custom-call(s32[12]{0:T(128)S(1)} %stack.51.sc, bf16[2048,128]{1,0:T(8,128)(2,1)S(1)} %constant_dynamic-update-slice_fusion.ka, bf16[2048,128]{1,0:T(8,128)(2,1)S(1)} %collective-permute-done.3.kb, ...), custom_call_target="tpu_custom_call" | custom-call | flops 1073741824 | bytes 2097152 | tf_op jit(solution)/shard_map/first/pallas_call | solution.py:346
  31.5 1.5 collective-permute-start.10
  33.1 5.9 %more1.1 = (f32[3,8,4096]{2,1,0:T(8,128)S(1)}, f32[2,4,4,128]{3,2,1,0:T(4,128)S(1)}) custom-call(s32[12]{0:T(128)S(1)} %stack.51.sc, bf16[4096,128]{1,0:T(8,128)(2,1)S(1)} %get-tuple-element.22.kp, f32[3,8,4096]{2,1,0:T(8,128)S(1)} %get-tuple-element.26.old, bf16[512,128]{1,0:T(8,128)(2,1)S(1)} %collective-permute-done.7.refs_0_.refs_1_, ...), custom_call_target="tpu_custom_call" | custom-call | flops 2147483648 | bytes 2097152 | tf_op jit(solution)/shard_map/more1/pallas_call | solution.py:346
  39.3 2.7 collective-permute-start.12
  41.9 5.9 %more3.1 = (f32[3,8,4096]{2,1,0:T(8,128)S(1)}, f32[2,4,4,128]{3,2,1,0:T(4,128)S(1)}) custom-call(s32[12]{0:T(128)S(1)} %stack.51.sc, bf16[4096,128]{1,0:T(8,128)(2,1)S(1)} %get-tuple-element.22.kp, f32[3,8,4096]{2,1,0:T(8,128)S(1)} %get-tuple-element.30.old, bf16[512,128]{1,0:T(8,128)(2,1)S(1)} %collective-permute-done.9.refs_0_.refs_3_, ...), custom_call_target="tpu_custom_call" | custom-call | flops 2147483648 | bytes 2097152 | tf_op jit(solution)/shard_map/more3/pallas_call | solution.py:346
  48.0 5.9 %more5.1 = (f32[3,8,4096]{2,1,0:T(8,128)S(1)}, f32[2,4,4,128]{3,2,1,0:T(4,128)S(1)}) custom-call(s32[12]{0:T(128)S(1)} %stack.51.sc, bf16[4096,128]{1,0:T(8,128)(2,1)S(1)} %get-tuple-element.22.kp, f32[3,8,4096]{2,1,0:T(8,128)S(1)} %get-tuple-element.32.old, bf16[512,128]{1,0:T(8,128)(2,1)S(1)} %collective-permute-done.11.refs_0_.refs_5_, ...), custom_call_target="tpu_custom_call" | custom-call | flops 2147483648 | bytes 2097152 | tf_op jit(solution)/shard_map/more5/pallas_call | solution.py:346
  53.8 221.2 %last.1 = (f32[32,4,128]{2,1,0:T(4,128)S(1)}, f32[8,4,512]{2,1,0:T(4,128)S(1)}) custom-call(s32[12]{0:T(128)S(1)} %stack.51.sc, bf16[4096,128]{1,0:T(8,128)(2,1)S(1)} %get-tuple-element.22.kp, f32[3,8,4096]{2,1,0:T(8,128)S(1)} %get-tuple-element.35.old, bf16[512,128]{1,0:T(8,128)(2,1)S(1)} %collective-permute-done.13.q.refs_7_, ...), custom_call_target="tpu_custom_call" | custom-call | flops 1073741824 | bytes 2097152 | tf_op jit(solution)/shard_map/last/pallas_call | solution.py:346
  275.0 12.1 %all_to_all.10.cols = f32[8,4,512]{2,1,0:T(4,128)S(1)} all-to-all(f32[8,4,512]{2,1,0:T(4,128)S(1)} %get-tuple-element.41), channel_id=1, replica_groups=mesh['zl'=2,'y'=4,'zh'=4,'x'=4,'core'=2] {'core','x'}, dimensions={0} | all-to-all | bytes 131072 | tf_op jit(solution)/shard_map/all_to_all | solution.py:396
  287.1 15.3 %all_to_all.11.rows = f32[32,4,128]{2,1,0:T(4,128)S(1)} all-to-all(f32[32,4,128]{2,1,0:T(4,128)S(1)} %get-tuple-element.40), channel_id=1, replica_groups=mesh['zl'=2,'y'=4,'zh'=4,'x'=4,'core'=2] {'zh','zl','y'}, dimensions={0} | all-to-all | bytes 131072 | tf_op jit(solution)/shard_map/all_to_all | solution.py:395
  302.4 1.4 finish.1
  (23 shorter events, 0.7 us)
Async XLA Ops:
  0.6 5.5 %collective-permute-start = (bf16[512,128]{1,0:T(8,128)(2,1)}, bf16[512,128]{1,0:T(8,128)(2,1)S(1)}, u32[]{:S(2)}, u32[]{:S(2)}) collective-permute-start(bf16[512,128]{1,0:T(8,128)(2,1)} %param.3), channel_id=1, source_target_pairs={{0,2},{1,3},{2,0},{3,1},{4,6},{5,7},{6,4},{7,5},{8,10},{9,11},{10,... | collective-permute-start | bytes 393224 | tf_op jit(solution)/shard_map/ppermute | solution.py:323
  2.8 5.2 %collective-permute-start.1 = (bf16[512,128]{1,0:T(8,128)(2,1)}, bf16[512,128]{1,0:T(8,128)(2,1)S(1)}, u32[]{:S(2)}, u32[]{:S(2)}) collective-permute-start(bf16[512,128]{1,0:T(8,128)(2,1)} %param.3), channel_id=1, source_target_pairs={{0,6},{1,7},{2,4},{3,5},{4,2},{5,3},{6,0},{7,1},{8,14},{9,15},{10,... | collective-permute-start | bytes 393224 | tf_op jit(solution)/shard_map/ppermute | solution.py:323
  4.6 6.5 %collective-permute-start.2 = (bf16[512,128]{1,0:T(8,128)(2,1)}, bf16[512,128]{1,0:T(8,128)(2,1)S(1)}, u32[]{:S(2)}, u32[]{:S(2)}) collective-permute-start(bf16[512,128]{1,0:T(8,128)(2,1)} %param.3), channel_id=1, source_target_pairs={{0,4},{1,5},{2,6},{3,7},{4,0},{5,1},{6,2},{7,3},{8,12},{9,13},{10,... | collective-permute-start | bytes 393224 | tf_op jit(solution)/shard_map/ppermute | solution.py:323
  8.0 5.4 %copy-start = (bf16[128,128]{1,0:T(8,128)(2,1)S(1)}, bf16[128,128]{1,0:T(8,128)(2,1)}, u32[]{:S(2)}) copy-start(bf16[128,128]{1,0:T(8,128)(2,1)} %param.2) | copy-start | bytes 98308
  11.1 15.2 %collective-permute-start.3 = (bf16[2048,128]{1,0:T(8,128)(2,1)S(1)}, bf16[2048,128]{1,0:T(8,128)(2,1)S(1)}, u32[]{:S(2)}, u32[]{:S(2)}) collective-permute-start(bf16[2048,128]{1,0:T(8,128)(2,1)S(1)} %constant_dynamic-update-slice_fusion.ka), channel_id=1, source_target_pairs={{0,1},{1,0},{2,3},{3,2},{4,5},{5,4},{6,7},{7,6},{8,9},{9,8},{10,11... | collective-permute-start | bytes 1572872 | tf_op jit(solution)/shard_map/ppermute | solution.py:323
  13.4 3.6 %collective-permute-start.4 = (bf16[128,128]{1,0:T(8,128)(2,1)S(1)}, bf16[128,128]{1,0:T(8,128)(2,1)S(1)}, u32[]{:S(2)}, u32[]{:S(2)}) collective-permute-start(bf16[128,128]{1,0:T(8,128)(2,1)S(1)} %copy-done), channel_id=1, source_target_pairs={{0,32},{1,33},{2,34},{3,35},{4,36},{5,37},{6,38},{7,39},{8,40},{9,... | collective-permute-start | bytes 98312 | tf_op jit(solution)/shard_map/ppermute | solution.py:323
  14.4 4.0 %collective-permute-start.5 = (bf16[128,128]{1,0:T(8,128)(2,1)S(1)}, bf16[128,128]{1,0:T(8,128)(2,1)S(1)}, u32[]{:S(2)}, u32[]{:S(2)}) collective-permute-start(bf16[128,128]{1,0:T(8,128)(2,1)S(1)} %copy-done), channel_id=1, source_target_pairs={{0,96},{1,97},{2,98},{3,99},{4,100},{5,101},{6,102},{7,103},{8,104... | collective-permute-start | bytes 98312 | tf_op jit(solution)/shard_map/ppermute | solution.py:323
  16.3 4.3 %collective-permute-start.6 = (bf16[128,128]{1,0:T(8,128)(2,1)S(1)}, bf16[128,128]{1,0:T(8,128)(2,1)S(1)}, u32[]{:S(2)}, u32[]{:S(2)}) collective-permute-start(bf16[128,128]{1,0:T(8,128)(2,1)S(1)} %copy-done), channel_id=1, source_target_pairs={{0,64},{1,65},{2,66},{3,67},{4,68},{5,69},{6,70},{7,71},{8,72},{9,... | collective-permute-start | bytes 98312 | tf_op jit(solution)/shard_map/ppermute | solution.py:323
  20.6 11.0 %collective-permute-start.7 = (bf16[512,128]{1,0:T(8,128)(2,1)S(1)}, bf16[512,128]{1,0:T(8,128)(2,1)S(1)}, u32[]{:S(2)}, u32[]{:S(2)}) collective-permute-start(bf16[512,128]{1,0:T(8,128)(2,1)S(1)} %constant_dynamic-update-slice_fusion.4.q.refs_0_), channel_id=1, source_target_pairs={{0,128},{1,129},{2,130},{3,131},{4,132},{5,133},{6,134},{7,135},{8... | collective-permute-start | bytes 393224 | tf_op jit(solution)/shard_map/ppermute | solution.py:333
  22.2 9.4 %collective-permute-start.8 = (bf16[512,128]{1,0:T(8,128)(2,1)S(1)}, bf16[512,128]{1,0:T(8,128)(2,1)S(1)}, u32[]{:S(2)}, u32[]{:S(2)}) collective-permute-start(bf16[512,128]{1,0:T(8,128)(2,1)S(1)} %constant_dynamic-update-slice_fusion.4.q.refs_0_), channel_id=1, source_target_pairs={{0,152},{1,153},{2,154},{3,155},{4,156},{5,157},{6,158},{7,159},{8... | collective-permute-start | bytes 393224 | tf_op jit(solution)/shard_map/ppermute | solution.py:333
  31.5 7.4 %collective-permute-start.10 = (bf16[512,128]{1,0:T(8,128)(2,1)S(1)}, bf16[512,128]{1,0:T(8,128)(2,1)S(1)}, u32[]{:S(2)}, u32[]{:S(2)}) collective-permute-start(bf16[512,128]{1,0:T(8,128)(2,1)S(1)} %collective-permute-done.8.refs_1_.refs_2_), channel_id=1, source_target_pairs={{0,152},{1,153},{2,154},{3,155},{4,156},{5,157},{6,158},{7,159},{8... | collective-permute-start | bytes 393224 | tf_op jit(solution)/shard_map/ppermute | solution.py:333
  33.0 6.0 %collective-permute-start.9 = (bf16[512,128]{1,0:T(8,128)(2,1)S(1)}, bf16[512,128]{1,0:T(8,128)(2,1)S(1)}, u32[]{:S(2)}, u32[]{:S(2)}) collective-permute-start(bf16[512,128]{1,0:T(8,128)(2,1)S(1)} %collective-permute-done.7.refs_0_.refs_1_), channel_id=1, source_target_pairs={{0,128},{1,129},{2,130},{3,131},{4,132},{5,133},{6,134},{7,135},{8... | collective-permute-start | bytes 393224 | tf_op jit(solution)/shard_map/ppermute | solution.py:333
  39.0 8.9 %collective-permute-start.11 = (bf16[512,128]{1,0:T(8,128)(2,1)S(1)}, bf16[512,128]{1,0:T(8,128)(2,1)S(1)}, u32[]{:S(2)}, u32[]{:S(2)}) collective-permute-start(bf16[512,128]{1,0:T(8,128)(2,1)S(1)} %collective-permute-done.9.refs_0_.refs_3_), channel_id=1, source_target_pairs={{0,128},{1,129},{2,130},{3,131},{4,132},{5,133},{6,134},{7,135},{8... | collective-permute-start | bytes 393224 | tf_op jit(solution)/shard_map/ppermute | solution.py:333
  39.3 8.6 %collective-permute-start.12 = (bf16[512,128]{1,0:T(8,128)(2,1)S(1)}, bf16[512,128]{1,0:T(8,128)(2,1)S(1)}, u32[]{:S(2)}, u32[]{:S(2)}) collective-permute-start(bf16[512,128]{1,0:T(8,128)(2,1)S(1)} %collective-permute-done.10.refs_1_.refs_4_), channel_id=1, source_target_pairs={{0,152},{1,153},{2,154},{3,155},{4,156},{5,157},{6,158},{7,159},{8... | collective-permute-start | bytes 393224 | tf_op jit(solution)/shard_map/ppermute | solution.py:333
  47.9 6.0 %collective-permute-start.13 = (bf16[512,128]{1,0:T(8,128)(2,1)S(1)}, bf16[512,128]{1,0:T(8,128)(2,1)S(1)}, u32[]{:S(2)}, u32[]{:S(2)}) collective-permute-start(bf16[512,128]{1,0:T(8,128)(2,1)S(1)} %collective-permute-done.11.refs_0_.refs_5_), channel_id=1, source_target_pairs={{0,128},{1,129},{2,130},{3,131},{4,132},{5,133},{6,134},{7,135},{8... | collective-permute-start | bytes 393224 | tf_op jit(solution)/shard_map/ppermute | solution.py:333

commit v3 on v2

--- a/solution.py
+++ b/solution.py
@@ -14,8 +14,8 @@
 BAND = 4096
 PIECE = 512
 RUN = 32
-ORDER = (0, 1, 3, 2)
 TILES = 4
+UNROLL = 4
 SCALE = math.log2(math.e) / math.sqrt(CH)
 LOW, HIGH = 2.0**-90, 2.0**100
 AXES = ("zl", "y", "zh", "x", "core")
@@ -64,7 +64,7 @@
 
 def query_weights(sc, z, half):
     r = iota((8, 128), 0)
-    slot = jnp.where(r < 4, ORDER[2 * half], ORDER[2 * half + 1])
+    slot = jnp.where(r < 4, 2 * half, 2 * half + 1)
     x, y = cell(query_base(z, sc[Y] ^ slot, sc[X], sc[CORE]) + (r & 3) * RUN)
     return x + (RUN - 256.0), y
 
@@ -76,7 +76,7 @@
 
 def set_keys(sc, ka, kb, kf, kp):
     for j in range(4):
-        slot = sc[X] ^ ORDER[j]
+        slot = sc[X] ^ j
         for core, ref in ((sc[CORE], ka), (1 - sc[CORE], kb)):
             at = pl.multiple_of((core * 4 + slot) * 512, 512)
             kf[pl.ds(at, 512), :] = ref[j * 512 : j * 512 + 512, :].astype(jnp.float32)
@@ -90,13 +90,13 @@
     lax.fori_loop(0, RUN, tile, 0, unroll=4)
 
 
-def set_queries(ref, qp):
+def set_queries(refs, qp):
     perm = run_order()
-    for half in range(2):
-        rows = slice(half * 256, half * 256 + 256)
-        qp[rows, :] = jnp.dot(perm, ref[rows, :], preferred_element_type=jnp.float32).astype(
-            jnp.bfloat16
-        )
+    for i, ref in enumerate(refs):
+        for half in range(2):
+            rows = slice(half * 256, half * 256 + 256)
+            got = jnp.dot(perm, ref[rows, :], preferred_element_type=jnp.float32)
+            qp[i * PIECE + half * 256 : i * PIECE + half * 256 + 256, :] = got.astype(jnp.bfloat16)
 
 
 def in_order(refs, part):
@@ -107,28 +107,29 @@
     return split2(jnp.concatenate(got, 0))
 
 
-def one_piece(sc, z, qp, kp, acc, sums_ref, moments_ref, store, tops=None):
+def block(sc, zs, qp, kp, acc, sums_ref, moments_ref, store, tops=None):
     tiles = TILES if tops is None else 1
+    halves = 2 * len(zs)
     sums_ref[...] = jnp.zeros_like(sums_ref)
     moments_ref[...] = jnp.zeros_like(moments_ref)
-    weights = [query_weights(sc, z, half) for half in range(2)]
+    weights = [query_weights(sc, zs[half // 2], half % 2) for half in range(halves)]
 
     def chunk(j, carry):
         at = pl.multiple_of(j * tiles * 128, tiles * 128)
         lanes = pl.ds(at, tiles * 128)
-        for half in range(2):
-            s = nt_dot(qp[half * 256 : half * 256 + 256, :], kp[lanes, :]) * SCALE
-            if tops is None:
-                for_query = for_key = jnp.exp2(s)
-            else:
-                for_query = jnp.exp2(s - tops[0][half * 256 : half * 256 + 256, :])
-                for_key = jnp.exp2(s - tops[1][0:1, lanes])
+        s = nt_dot(qp[0 : halves * 256, :], kp[lanes, :]) * SCALE
+        if tops is None:
+            for_query = for_key = jnp.exp2(s)
+        else:
+            for_query = jnp.exp2(s - tops[0][...])
+            for_key = jnp.exp2(s - tops[1][0:1, lanes])
+        for half in range(halves):
             sums, moments = [None] * tiles, [None] * tiles
             for u in range(RUN):
                 rows = slice(half * 256 + u * 8, half * 256 + u * 8 + 8)
                 own_sum, own_moment = sums_ref[rows, :], moments_ref[rows, :]
                 for i in range(tiles):
-                    part = (slice(u * 8, u * 8 + 8), slice(i * 128, i * 128 + 128))
+                    part = (rows, slice(i * 128, i * 128 + 128))
                     e = for_key[part]
                     sums[i] = e if u == 0 else sums[i] + e
                     moments[i] = sums[i] if u == 0 else moments[i] + sums[i]
@@ -144,71 +145,74 @@
                 acc[2, :, d] += sums[i] * y
         return carry
 
-    count = BAND // 128 // tiles
-    lax.fori_loop(0, count, chunk, 0, unroll=4 if tops is None else 1)
+    lax.fori_loop(0, BAND // 128 // tiles, chunk, 0, unroll=UNROLL if tops is None else 1)
     w = key_weights(sc)
-    for slot in range(4):
-        hi, lo = in_order((sums_ref, moments_ref), slot)
-        got = nt_dot(w, hi) + nt_dot(w, lo)
-        store(slot, slice(0, 3), got[0:3])
-
-
-def spread_keys(col_ref, acc, top=None):
+    for piece in range(len(zs)):
+        for slot in range(4):
+            hi, lo = in_order((sums_ref, moments_ref), 4 * piece + slot)
+            store(piece, slot, slice(0, 3), (nt_dot(w, hi) + nt_dot(w, lo))[0:3])
+
+
+def spread_keys(sc, near, far, spread, acc, top=None):
     lane = iota((8, 128), 1) >> 4
     for stat in range(4):
         if stat == 3 and top is None:
-            col_ref[:, 3:4, :] = jnp.zeros((8, 1, 512), jnp.float32)
+            near[:, 3:4, :] = jnp.zeros((4, 1, 512), jnp.float32)
+            far[:, 3:4, :] = jnp.zeros((4, 1, 512), jnp.float32)
             continue
-        for block in range(4):
+        for part in range(4):
             out = jnp.zeros((8, 128), jnp.float32)
             for t in range(8):
-                d = slice((block * 8 + t) * 128, (block * 8 + t) * 128 + 128)
+                d = slice((part * 8 + t) * 128, (part * 8 + t) * 128 + 128)
                 value = top[0:1, d] if stat == 3 else jnp.sum(acc[stat, :, d], 0, keepdims=True)
                 value = pltpu.roll(jnp.broadcast_to(value, (8, 128)), 0, 1, stride=16, stride_axis=0)
                 out = jnp.where(lane == t, pltpu.roll(value, (t * 16 + 16) % 128, 1), out)
-            for s in range(8):
-                lanes = slice(block * 128, block * 128 + 128)
-                col_ref[s, stat : stat + 1, lanes] = out[7 - s : 8 - s, :]
+            spread[:, part * 128 : part * 128 + 128] = out
+        for i, ref in enumerate((near, far)):
+            for j in range(4):
+                row = 7 - ((sc[CORE] ^ i) * 4 + (sc[X] ^ j))
+                ref[j, stat : stat + 1, :] = spread[pl.ds(row, 1), :]
 
 
 def first_kernel(sc, ka, kb, q, kp, acc, rows, kf, qp, sums_ref, moments_ref):
     set_keys(sc, ka, kb, kf, kp)
     acc[...] = jnp.zeros_like(acc)
-    set_queries(q, qp)
-
-    def store(slot, stats, value):
-        rows[0, slot, stats, :] = value
-
-    one_piece(sc, sc[PIECE_Z], qp, kp, acc, sums_ref, moments_ref, store)
+    set_queries([q], qp)
+
+    def store(piece, slot, stats, value):
+        rows[piece, slot, stats, :] = value
+
+    block(sc, [sc[PIECE_Z]], qp, kp, acc, sums_ref, moments_ref, store)
 
 
 def more_kernel(first, sc, kp, old, *refs):
-    count = (len(refs) - 5) // 1
+    count = len(refs) - 5
     qs, (acc, rows, qp, sums_ref, moments_ref) = refs[:count], refs[count:]
     acc[...] = old[...]
-    for i, q in enumerate(qs):
-        set_queries(q, qp)
-
-        def store(slot, stats, value, i=i):
-            rows[i, slot, stats, :] = value
-
-        one_piece(sc, sc[PIECE_Z + first + i], qp, kp, acc, sums_ref, moments_ref, store)
+    set_queries(qs, qp)
+
+    def store(piece, slot, stats, value):
+        rows[piece, slot, stats, :] = value
+
+    zs = [sc[PIECE_Z + first + i] for i in range(count)]
+    block(sc, zs, qp, kp, acc, sums_ref, moments_ref, store)
 
 
 def last_kernel(sc, kp, old, q, r0, r1, r2, r3, *refs):
     pieces, refs = refs[:8], refs[8:]
-    row_ref, col_ref, acc, qp, sums_ref, moments_ref, rm, km, raw, sem = refs
+    row_ref, near, far, acc, qp, sums_ref, moments_ref, spread, rm, km, raw, sem = refs
     acc[...] = old[...]
-    set_queries(q, qp)
+    set_queries([q], qp)
 
     def place(piece, slot):
-        return sc[PIECE_Z + piece] * 4 + (sc[Y] ^ ORDER[slot])
+        return sc[PIECE_Z + piece] * 4 + (sc[Y] ^ slot)
 
     def store(piece, slot, stats, value):
         row_ref[place(piece, slot), stats, :] = value
 
-    one_piece(
-        sc, sc[PIECE_Z + 7], qp, kp, acc, sums_ref, moments_ref, functools.partial(store, 7)
+    block(
+        sc, [sc[PIECE_Z + 7]], qp, kp, acc, sums_ref, moments_ref,
+        lambda _, *what: store(7, *what),
     )
     piece = 0
     for ref in (r0, r1, r2, r3):
@@ -217,10 +221,10 @@
                 store(piece, slot, slice(0, 3), ref[i, slot, 0:3, :])
             piece += 1
     row_ref[:, 3:4, :] = jnp.zeros((32, 1, 128), jnp.float32)
-    spread_keys(col_ref, acc)
-    row_sums, col_sums = row_ref[:, 0, :], col_ref[:, 0, :]
-    low = jnp.minimum(jnp.min(row_sums), jnp.min(col_sums))
-    high = jnp.maximum(jnp.max(row_sums), jnp.max(col_sums))
+    spread_keys(sc, near, far, spread, acc)
+    sums = [row_ref[:, 0, :], near[:, 0, :], far[:, 0, :]]
+    low = functools.reduce(jnp.minimum, [jnp.min(v) for v in sums])
+    high = functools.reduce(jnp.maximum, [jnp.max(v) for v in sums])
 
     @pl.when(jnp.logical_not((low > LOW) & (high < HIGH)))
     def _():
@@ -233,7 +237,7 @@
             copy = pltpu.make_async_copy(pieces[piece], raw, sem)
             copy.start()
             copy.wait()
-            set_queries(raw, qp)
+            set_queries([raw], qp)
 
         def block_top(half, t):
             lanes = pl.ds(pl.multiple_of(t * 128, 128), 128)
@@ -267,25 +271,31 @@
             for slot in range(4):
                 hi, lo = in_order((rm,), slot)
                 store(piece, slot, slice(3, 4), (nt_dot(pick, hi) + nt_dot(pick, lo))[0:1])
-            one_piece(
-                sc, sc[PIECE_Z + piece], qp, kp, acc, sums_ref, moments_ref,
-                functools.partial(store, piece), (rm, km),
+            block(
+                sc, [sc[PIECE_Z + piece]], qp, kp, acc, sums_ref, moments_ref,
+                lambda _, *what, piece=piece: store(piece, *what), (rm, km),
             )
-        spread_keys(col_ref, acc, km)
-
-
-def final_kernel(sc, rows, cols, f_ref, b_ref):
-    def merged(parts):
-        top = parts[0][3:4]
-        for part in parts[1:]:
-            top = jnp.maximum(top, part[3:4])
-        return sum(part[0:3] * jnp.exp2(part[3:4] - top) for part in parts)
-
-    q = merged([rows[j] for j in range(32)])
+        spread_keys(sc, near, far, spread, acc, km)
+
+
+def merged(parts):
+    top = parts[0][3:4]
+    for part in parts[1:]:
+        top = jnp.maximum(top, part[3:4])
+    return sum(part[0:3] * jnp.exp2(part[3:4] - top) for part in parts), top
+
+
+def merge_kernel(a, b, *outs):
+    for j, out in enumerate(outs):
+        out[0:3, :], out[3:4, :] = merged([a[j], b[j]])
+
+
+def final_kernel(sc, rows, k0, k1, k2, k3, f_ref, b_ref):
+    q, _ = merged([rows[j] for j in range(32)])
     x, y = cell(query_base(sc[Z], sc[Y], sc[X], sc[CORE]) + iota((1, 128), 1))
     f_ref[0:1, :] = (q[1:2] / q[0:1] + (256.0 - x)) / FRAME_W
     f_ref[1:2, :] = (q[2:3] / q[0:1] + (128.0 - y)) / FRAME_W
-    k = merged([cols[j] for j in range(8)])
+    k, _ = merged([ref[...] for ref in (k0, k1, k2, k3)])
     lane = iota((1, 512), 1)
     x, y = cell(key_base(sc[Z], sc[Y], sc[X], sc[CORE]) + (lane & 15) * RUN + (lane >> 4))
     bx = (k[1:2] / k[0:1] + (256.0 - x)) / FRAME_W
@@ -361,14 +371,18 @@
 def on_device(q, k):
     me = {name: lax.axis_index(name) for name in AXES}
     z = me["zh"] * 2 + me["zl"]
-    ka = jnp.concatenate([k] + [swap(k, x=j) for j in ORDER[1:]])
-    own = jnp.concatenate([q] + [swap(q, y=j) for j in ORDER[1:]])
+    by_y = [swap(q, y=j) for j in (1, 3, 2)]
+    by_x = [swap(k, x=j) for j in (1, 3, 2)]
+    by_y, by_x = lax.optimization_barrier((by_y, by_x))
+    own = jnp.concatenate([q, by_y[0], by_y[2], by_y[1]])
+    ka = jnp.concatenate([k, by_x[0], by_x[2], by_x[1]])
     kb = swap(ka, core=1)
     z_of = [(z + off) % 8 for off in (0, -1, 1, -2, 2, -3, 3, -4)]
     sc = jnp.stack([me["core"], me["x"], me["y"], z] + z_of).astype(jnp.int32)
 
     half_sums = [pltpu.VMEM((PIECE, 128), jnp.float32)] * 2
     piece_rows = pltpu.VMEM((PIECE, CH), jnp.bfloat16)
+    two = [pltpu.VMEM((2 * PIECE, CH), jnp.bfloat16)] + [pltpu.VMEM((2 * PIECE, 128), jnp.float32)] * 2
     pieces = [own, ring(own, 1), ring(own, -1)]
     kp, acc, r0 = call(
         first_kernel, "first", (sc, ka, kb, own), [SMEM, VMEM, VMEM, VMEM],
@@ -382,20 +396,23 @@
         acc, got = call(
             functools.partial(more_kernel, first), f"more{first}",
             (sc, kp, acc, up, down), [SMEM] + [VMEM] * 4,
-            [f32(3, 8, BAND), f32(2, 4, 4, 128)], [piece_rows] + half_sums, 2,
+            [f32(3, 8, BAND), f32(2, 4, 4, 128)], two, 2,
         )
         parts.append(got)
-    rows, cols = call(
+    rows, near, far = call(
         last_kernel, "last", (sc, kp, acc, pieces[7], *parts, *pieces),
-        [SMEM] + [VMEM] * 7 + [ANY] * 8, [f32(32, 4, 128), f32(8, 4, 512)],
+        [SMEM] + [VMEM] * 7 + [ANY] * 8, [f32(32, 4, 128), f32(4, 4, 512), f32(4, 4, 512)],
         [pltpu.VMEM((3, 8, BAND), jnp.float32), piece_rows] + half_sums
-        + [pltpu.VMEM((PIECE, 128), jnp.float32), pltpu.VMEM((8, BAND), jnp.float32),
-           piece_rows, pltpu.SemaphoreType.DMA], 1,
-    )
+        + [pltpu.VMEM((8, 512), jnp.float32), pltpu.VMEM((PIECE, 128), jnp.float32),
+           pltpu.VMEM((8, BAND), jnp.float32), piece_rows, pltpu.SemaphoreType.DMA], 1,
+    )
+    cols = call(
+        merge_kernel, "merge", (near, swap(far, core=1)), [VMEM] * 2, [f32(4, 512)] * 4, [], 0
+    )
+    cols = [cols[0]] + [swap(cols[j], x=j) for j in (1, 3, 2)]
     rows = lax.all_to_all(rows, ("zh", "zl", "y"), 0, 0)
-    cols = lax.all_to_all(cols, ("core", "x"), 0, 0)
     return call(
-        final_kernel, "finish", (sc, rows, cols), [SMEM, VMEM, VMEM], [f32(2, 128), f32(2, 512)], [], 0
+        final_kernel, "finish", (sc, rows, *cols), [SMEM] + [VMEM] * 5, [f32(2, 128), f32(2, 512)], [], 0
     )
 
 

time: 304 us -> 290 us (0.954)
  blocking collectives: 27.4 us -> 0 us
  starting transfers between devices: 20.8 us -> 34.9 us
    all_to_all x2 -> x0, blocking collectives: 27.4 us -> none  [the longest x1 15.3 us: on_device(): rows = lax.all_to_all(rows, ('zh', 'zl', 'y'), 0, 0)]
    ppermute x7 -> x11, starting transfers between devices: 10.5 us -> 17.7 us  [swap(): return lax.ppermute(value, AXES, [(i, partner(i)) for i in range(256)])]
    all_to_all x0 -> x1, starting transfers between devices: none -> 6.83 us  [on_device(): rows = lax.all_to_all(rows, ('zh', 'zl', 'y'), 0, 0)]
    pallas_call x6 -> x7, Pallas kernels: 245 us -> 245 us  [call(): pl.pallas_call(kernel, name=name, out_shape=out_shape, in_specs=in_specs,...]
    ppermute x7 -> x11, waiting for transfers between devices: 8.33 us -> 7.47 us  [swap(): return lax.ppermute(value, AXES, [(i, partner(i)) for i in range(256)])]
  transfers between devices with their start and end apart: 14 -> 19, of which waited for: 4 -> 5; matrix products, arithmetic and copies ran while one was open for 0% -> 0% of each run, Pallas kernels for 8% -> 7%
where the time goes in v3:
time: 290 us; the launch traced here: 289 us
  Pallas kernels  245 us (84%)
  starting transfers between devices  34.9 us (12%)
  waiting for transfers between devices  7.49 us (3%)
    pallas_call x7, Pallas kernels, call(): pl.pallas_call(kernel, name=name, out_shape=out_shape, in_specs=in_specs,...  245 us
    ppermute x11, starting transfers between devices, swap(): return lax.ppermute(value, AXES, [(i, partner(i)) for i in range(256)])  17.7 us
    ppermute x7, starting transfers between devices, ring(): return lax.ppermute(value, AXES, [(i, partner(i)) for i in range(256)])  10.3 us
    ppermute x11, waiting for transfers between devices, swap(): return lax.ppermute(value, AXES, [(i, partner(i)) for i in range(256)])  7.47 us
    all_to_all x1, starting transfers between devices, on_device(): rows = lax.all_to_all(rows, ('zh', 'zl', 'y'), 0, 0)  6.83 us
  transfers between devices with their start and end apart: 19, of which 5 were waited for; matrix products, arithmetic and copies ran while one was open for 0% of the time, Pallas kernels for 7%

profile of v3, /device:TPU:1, one launch (start us, length us, event | category | flops | bytes accessed | tf_op | source)
XLA Modules:
  0.0 288.8 jit_solution(14526654298442842872)
XLA Ops:
  0.6 2.2 collective-permute-start
  2.8 1.2 collective-permute-start.3
  4.1 1.8 collective-permute-start.4
  6.5 1.9 collective-permute-start.1
  9.1 0.9 constant_dynamic-update-slice_fusion.3
  10.1 0.9 collective-permute-done.1
  11.0 2.2 collective-permute-done.2
  13.3 2.7 collective-permute-start.6
  16.1 1.7 collective-permute-start.7
  17.8 4.0 %collective-permute-start.8 = (bf16[512,128]{1,0:T(8,128)(2,1)S(1)}, bf16[512,128]{1,0:T(8,128)(2,1)S(1)}, u32[]{:S(2)}, u32[]{:S(2)}) collective-permute-start(bf16[512,128]{1,0:T(8,128)(2,1)S(1)} %constant_dynamic-update-slice_fusion.4.q.refs_0_), channel_id=1, source_target_pairs={{0,152},{1,153},{2,154},{3,155},{4,156},{5,157},{6,158},{7,159},{8... | collective-permute-start | bytes 393224 | tf_op jit(solution)/shard_map/ppermute | solution.py:343
  21.9 5.2 %first.1 = (bf16[4096,128]{1,0:T(8,128)(2,1)S(1)}, f32[3,8,4096]{2,1,0:T(8,128)S(1)}, f32[1,4,4,128]{3,2,1,0:T(4,128)S(1)}) custom-call(s32[12]{0:T(128)S(1)} %stack.51.sc, bf16[2048,128]{1,0:T(8,128)(2,1)S(1)} %constant_dynamic-update-slice_fusion.ka, bf16[2048,128]{1,0:T(8,128)(2,1)S(1)} %collective-permute-done.6.kb, ...), custom_call_target="tpu_custom_call" | custom-call | flops 1073741824 | bytes 2097152 | tf_op jit(solution)/shard_map/first/pallas_call | solution.py:356
  27.2 1.5 collective-permute-start.10
  28.7 5.4 %more1.1 = (f32[3,8,4096]{2,1,0:T(8,128)S(1)}, f32[2,4,4,128]{3,2,1,0:T(4,128)S(1)}) custom-call(s32[12]{0:T(128)S(1)} %stack.51.sc, bf16[4096,128]{1,0:T(8,128)(2,1)S(1)} %get-tuple-element.39.kp, f32[3,8,4096]{2,1,0:T(8,128)S(1)} %get-tuple-element.43.old, bf16[512,128]{1,0:T(8,128)(2,1)S(1)} %collective-permute-done.7.refs_0_.refs_1_, ...), custom_call_target="tpu_custom_call" | custom-call | flops 2147483648 | bytes 2097152 | tf_op jit(solution)/shard_map/more1/pallas_call | solution.py:356
  34.4 2.7 collective-permute-start.12
  37.1 5.4 %more3.1 = (f32[3,8,4096]{2,1,0:T(8,128)S(1)}, f32[2,4,4,128]{3,2,1,0:T(4,128)S(1)}) custom-call(s32[12]{0:T(128)S(1)} %stack.51.sc, bf16[4096,128]{1,0:T(8,128)(2,1)S(1)} %get-tuple-element.39.kp, f32[3,8,4096]{2,1,0:T(8,128)S(1)} %get-tuple-element.47.old, bf16[512,128]{1,0:T(8,128)(2,1)S(1)} %collective-permute-done.9.refs_0_.refs_3_, ...), custom_call_target="tpu_custom_call" | custom-call | flops 2147483648 | bytes 2097152 | tf_op jit(solution)/shard_map/more3/pallas_call | solution.py:356
  42.5 5.4 %more5.1 = (f32[3,8,4096]{2,1,0:T(8,128)S(1)}, f32[2,4,4,128]{3,2,1,0:T(4,128)S(1)}) custom-call(s32[12]{0:T(128)S(1)} %stack.51.sc, bf16[4096,128]{1,0:T(8,128)(2,1)S(1)} %get-tuple-element.39.kp, f32[3,8,4096]{2,1,0:T(8,128)S(1)} %get-tuple-element.49.old, bf16[512,128]{1,0:T(8,128)(2,1)S(1)} %collective-permute-done.11.refs_0_.refs_5_, ...), custom_call_target="tpu_custom_call" | custom-call | flops 2147483648 | bytes 2097152 | tf_op jit(solution)/shard_map/more5/pallas_call | solution.py:356
  47.9 221.8 %last.1 = (f32[32,4,128]{2,1,0:T(4,128)}, f32[4,4,512]{2,1,0:T(4,128)S(1)}, f32[4,4,512]{2,1,0:T(4,128)S(1)}) custom-call(s32[12]{0:T(128)S(1)} %stack.51.sc, bf16[4096,128]{1,0:T(8,128)(2,1)S(1)} %get-tuple-element.39.kp, f32[3,8,4096]{2,1,0:T(8,128)S(1)} %get-tuple-element.52.old, bf16[512,128]{1,0:T(8,128)(2,1)S(1)} %collective-permute-done.13.q.refs_7_, ...), custom_call_target="tpu_custom_call" | custom-call | flops 1073741824 | bytes 2097152 | tf_op jit(solution)/shard_map/last/pallas_call | solution.py:356
  269.7 6.8 %all-to-all-start = ((f32[32,4,128]{2,1,0:T(4,128)}), f32[32,4,128]{2,1,0:T(4,128)S(1)}, u32[]{:S(2)}, u32[]{:S(2)}) async-start(f32[32,4,128]{2,1,0:T(4,128)} %get-tuple-element.57), calls=%async_computation | async-start | bytes 131072 | tf_op jit(solution)/shard_map/all_to_all | solution.py:413
  276.6 3.2 %collective-permute-start.14 = (f32[4,4,512]{2,1,0:T(4,128)S(1)}, f32[4,4,512]{2,1,0:T(4,128)S(1)}, u32[]{:S(2)}, u32[]{:S(2)}) collective-permute-start(f32[4,4,512]{2,1,0:T(4,128)S(1)} %get-tuple-element.59), channel_id=1, source_target_pairs={{0,1},{1,0},{2,3},{3,2},{4,5},{5,4},{6,7},{7,6},{8,9},{9,8},{10,11... | collective-permute-start | bytes 98312 | tf_op jit(solution)/shard_map/ppermute | solution.py:333
  279.7 0.9 collective-permute-done.14.b
  281.3 1.8 collective-permute-start.16
  284.0 1.4 collective-permute-done.16.k2
  285.3 2.1 collective-permute-done.17.k3
  287.4 1.4 finish.1
  (32 shorter events, 3.6 us)
Async XLA Ops:
  0.6 7.8 %collective-permute-start = (bf16[128,128]{1,0:T(8,128)(2,1)}, bf16[128,128]{1,0:T(8,128)(2,1)S(1)}, u32[]{:S(2)}, u32[]{:S(2)}) collective-permute-start(bf16[128,128]{1,0:T(8,128)(2,1)} %param.2), channel_id=1, source_target_pairs={{0,32},{1,33},{2,34},{3,35},{4,36},{5,37},{6,38},{7,39},{8,40},{9,... | collective-permute-start | bytes 98312 | tf_op jit(solution)/shard_map/ppermute | solution.py:333
  2.8 10.3 %collective-permute-start.3 = (bf16[512,128]{1,0:T(8,128)(2,1)}, bf16[512,128]{1,0:T(8,128)(2,1)S(1)}, u32[]{:S(2)}, u32[]{:S(2)}) collective-permute-start(bf16[512,128]{1,0:T(8,128)(2,1)} %param.3), channel_id=1, source_target_pairs={{0,2},{1,3},{2,0},{3,1},{4,6},{5,7},{6,4},{7,5},{8,10},{9,11},{10,... | collective-permute-start | bytes 393224 | tf_op jit(solution)/shard_map/ppermute | solution.py:333
  4.1 9.1 %collective-permute-start.4 = (bf16[512,128]{1,0:T(8,128)(2,1)}, bf16[512,128]{1,0:T(8,128)(2,1)S(1)}, u32[]{:S(2)}, u32[]{:S(2)}) collective-permute-start(bf16[512,128]{1,0:T(8,128)(2,1)} %param.3), channel_id=1, source_target_pairs={{0,6},{1,7},{2,4},{3,5},{4,2},{5,3},{6,0},{7,1},{8,14},{9,15},{10,... | collective-permute-start | bytes 393224 | tf_op jit(solution)/shard_map/ppermute | solution.py:333
  5.9 7.3 %collective-permute-start.5 = (bf16[512,128]{1,0:T(8,128)(2,1)}, bf16[512,128]{1,0:T(8,128)(2,1)S(1)}, u32[]{:S(2)}, u32[]{:S(2)}) collective-permute-start(bf16[512,128]{1,0:T(8,128)(2,1)} %param.3), channel_id=1, source_target_pairs={{0,4},{1,5},{2,6},{3,7},{4,0},{5,1},{6,2},{7,3},{8,12},{9,13},{10,... | collective-permute-start | bytes 393224 | tf_op jit(solution)/shard_map/ppermute | solution.py:333
  6.5 4.5 %collective-permute-start.1 = (bf16[128,128]{1,0:T(8,128)(2,1)}, bf16[128,128]{1,0:T(8,128)(2,1)S(1)}, u32[]{:S(2)}, u32[]{:S(2)}) collective-permute-start(bf16[128,128]{1,0:T(8,128)(2,1)} %param.2), channel_id=1, source_target_pairs={{0,96},{1,97},{2,98},{3,99},{4,100},{5,101},{6,102},{7,103},{8,104... | collective-permute-start | bytes 98312 | tf_op jit(solution)/shard_map/ppermute | solution.py:333
  8.4 4.8 %collective-permute-start.2 = (bf16[128,128]{1,0:T(8,128)(2,1)}, bf16[128,128]{1,0:T(8,128)(2,1)S(1)}, u32[]{:S(2)}, u32[]{:S(2)}) collective-permute-start(bf16[128,128]{1,0:T(8,128)(2,1)} %param.2), channel_id=1, source_target_pairs={{0,64},{1,65},{2,66},{3,67},{4,68},{5,69},{6,70},{7,71},{8,72},{9,... | collective-permute-start | bytes 98312 | tf_op jit(solution)/shard_map/ppermute | solution.py:333
  13.3 2.8 copy-start
  13.3 8.6 %collective-permute-start.6 = (bf16[2048,128]{1,0:T(8,128)(2,1)S(1)}, bf16[2048,128]{1,0:T(8,128)(2,1)S(1)}, u32[]{:S(2)}, u32[]{:S(2)}) collective-permute-start(bf16[2048,128]{1,0:T(8,128)(2,1)S(1)} %constant_dynamic-update-slice_fusion.ka), channel_id=1, source_target_pairs={{0,1},{1,0},{2,3},{3,2},{4,5},{5,4},{6,7},{7,6},{8,9},{9,8},{10,11... | collective-permute-start | bytes 1572872 | tf_op jit(solution)/shard_map/ppermute | solution.py:333
  16.1 11.1 %collective-permute-start.7 = (bf16[512,128]{1,0:T(8,128)(2,1)S(1)}, bf16[512,128]{1,0:T(8,128)(2,1)S(1)}, u32[]{:S(2)}, u32[]{:S(2)}) collective-permute-start(bf16[512,128]{1,0:T(8,128)(2,1)S(1)} %constant_dynamic-update-slice_fusion.4.q.refs_0_), channel_id=1, source_target_pairs={{0,128},{1,129},{2,130},{3,131},{4,132},{5,133},{6,134},{7,135},{8... | collective-permute-start | bytes 393224 | tf_op jit(solution)/shard_map/ppermute | solution.py:343
  17.8 9.4 %collective-permute-start.8 = (bf16[512,128]{1,0:T(8,128)(2,1)S(1)}, bf16[512,128]{1,0:T(8,128)(2,1)S(1)}, u32[]{:S(2)}, u32[]{:S(2)}) collective-permute-start(bf16[512,128]{1,0:T(8,128)(2,1)S(1)} %constant_dynamic-update-slice_fusion.4.q.refs_0_), channel_id=1, source_target_pairs={{0,152},{1,153},{2,154},{3,155},{4,156},{5,157},{6,158},{7,159},{8... | collective-permute-start | bytes 393224 | tf_op jit(solution)/shard_map/ppermute | solution.py:343
  27.2 6.9 %collective-permute-start.10 = (bf16[512,128]{1,0:T(8,128)(2,1)S(1)}, bf16[512,128]{1,0:T(8,128)(2,1)S(1)}, u32[]{:S(2)}, u32[]{:S(2)}) collective-permute-start(bf16[512,128]{1,0:T(8,128)(2,1)S(1)} %collective-permute-done.8.refs_1_.refs_2_), channel_id=1, source_target_pairs={{0,152},{1,153},{2,154},{3,155},{4,156},{5,157},{6,158},{7,159},{8... | collective-permute-start | bytes 393224 | tf_op jit(solution)/shard_map/ppermute | solution.py:343
  28.6 5.5 %collective-permute-start.9 = (bf16[512,128]{1,0:T(8,128)(2,1)S(1)}, bf16[512,128]{1,0:T(8,128)(2,1)S(1)}, u32[]{:S(2)}, u32[]{:S(2)}) collective-permute-start(bf16[512,128]{1,0:T(8,128)(2,1)S(1)} %collective-permute-done.7.refs_0_.refs_1_), channel_id=1, source_target_pairs={{0,128},{1,129},{2,130},{3,131},{4,132},{5,133},{6,134},{7,135},{8... | collective-permute-start | bytes 393224 | tf_op jit(solution)/shard_map/ppermute | solution.py:343
  34.1 8.3 %collective-permute-start.11 = (bf16[512,128]{1,0:T(8,128)(2,1)S(1)}, bf16[512,128]{1,0:T(8,128)(2,1)S(1)}, u32[]{:S(2)}, u32[]{:S(2)}) collective-permute-start(bf16[512,128]{1,0:T(8,128)(2,1)S(1)} %collective-permute-done.9.refs_0_.refs_3_), channel_id=1, source_target_pairs={{0,128},{1,129},{2,130},{3,131},{4,132},{5,133},{6,134},{7,135},{8... | collective-permute-start | bytes 393224 | tf_op jit(solution)/shard_map/ppermute | solution.py:343
  34.4 8.0 %collective-permute-start.12 = (bf16[512,128]{1,0:T(8,128)(2,1)S(1)}, bf16[512,128]{1,0:T(8,128)(2,1)S(1)}, u32[]{:S(2)}, u32[]{:S(2)}) collective-permute-start(bf16[512,128]{1,0:T(8,128)(2,1)S(1)} %collective-permute-done.10.refs_1_.refs_4_), channel_id=1, source_target_pairs={{0,152},{1,153},{2,154},{3,155},{4,156},{5,157},{6,158},{7,159},{8... | collective-permute-start | bytes 393224 | tf_op jit(solution)/shard_map/ppermute | solution.py:343
  42.4 5.5 %collective-permute-start.13 = (bf16[512,128]{1,0:T(8,128)(2,1)S(1)}, bf16[512,128]{1,0:T(8,128)(2,1)S(1)}, u32[]{:S(2)}, u32[]{:S(2)}) collective-permute-start(bf16[512,128]{1,0:T(8,128)(2,1)S(1)} %collective-permute-done.11.refs_0_.refs_5_), channel_id=1, source_target_pairs={{0,128},{1,129},{2,130},{3,131},{4,132},{5,133},{6,134},{7,135},{8... | collective-permute-start | bytes 393224 | tf_op jit(solution)/shard_map/ppermute | solution.py:343
  269.7 17.7 %all-to-all-start = ((f32[32,4,128]{2,1,0:T(4,128)}), f32[32,4,128]{2,1,0:T(4,128)S(1)}, u32[]{:S(2)}, u32[]{:S(2)}) async-start(f32[32,4,128]{2,1,0:T(4,128)} %get-tuple-element.57), calls=%async_computation | async-start | bytes 131072 | tf_op jit(solution)/shard_map/all_to_all | solution.py:413
  276.6 4.0 %collective-permute-start.14 = (f32[4,4,512]{2,1,0:T(4,128)S(1)}, f32[4,4,512]{2,1,0:T(4,128)S(1)}, u32[]{:S(2)}, u32[]{:S(2)}) collective-permute-start(f32[4,4,512]{2,1,0:T(4,128)S(1)} %get-tuple-element.59), channel_id=1, source_target_pairs={{0,1},{1,0},{2,3},{3,2},{4,5},{5,4},{6,7},{7,6},{8,9},{9,8},{10,11... | collective-permute-start | bytes 98312 | tf_op jit(solution)/shard_map/ppermute | solution.py:333
  280.6 3.3 %collective-permute-start.15 = (f32[4,512]{1,0:T(4,128)S(1)}, f32[4,512]{1,0:T(4,128)S(1)}, u32[]{:S(2)}, u32[]{:S(2)}) collective-permute-start(f32[4,512]{1,0:T(4,128)S(1)} %get-tuple-element.61), channel_id=1, source_target_pairs={{0,2},{1,3},{2,0},{3,1},{4,6},{5,7},{6,4},{7,5},{8,10},{9,11},{10,... | collective-permute-start | bytes 24584 | tf_op jit(solution)/shard_map/ppermute | solution.py:333
  281.3 4.0 %collective-permute-start.16 = (f32[4,512]{1,0:T(4,128)S(1)}, f32[4,512]{1,0:T(4,128)S(1)}, u32[]{:S(2)}, u32[]{:S(2)}) collective-permute-start(f32[4,512]{1,0:T(4,128)S(1)} %get-tuple-element.62), channel_id=1, source_target_pairs={{0,6},{1,7},{2,4},{3,5},{4,2},{5,3},{6,0},{7,1},{8,14},{9,15},{10,... | collective-permute-start | bytes 24584 | tf_op jit(solution)/shard_map/ppermute | solution.py:333
  283.1 4.3 %collective-permute-start.17 = (f32[4,512]{1,0:T(4,128)S(1)}, f32[4,512]{1,0:T(4,128)S(1)}, u32[]{:S(2)}, u32[]{:S(2)}) collective-permute-start(f32[4,512]{1,0:T(4,128)S(1)} %get-tuple-element.63), channel_id=1, source_target_pairs={{0,4},{1,5},{2,6},{3,7},{4,0},{5,1},{6,2},{7,3},{8,12},{9,13},{10,... | collective-permute-start | bytes 24584 | tf_op jit(solution)/shard_map/ppermute | solution.py:333
